TPU v7x, 256 devices: a whole 4x4x8 slice. The times are simulated.
256 devices in a mesh: expert: 64 (over z, x, core), dp: 4 (over y).
Axes of the slice: x: 4, y: 4, z: 8, core: 2. Of those that a mesh axis runs over, the one named last changes fastest.
Arguments:
- features: bfloat16 [32768, 32, 64], P(('expert', 'dp')), may hold values from -1 to 1
- spacing: float32 [32768, 32], P(('expert', 'dp')), may hold values from 0.02 to 0.3
- targets: float32 [3, 32768], P(None, ('expert', 'dp')), may hold values from 0 to 1
- ray_length: int32 [32768], P(('expert', 'dp')), may hold values from 1 to 32, as said below
- cell_id: int32 [32768, 32], P(('expert', 'dp')), may hold values from 0 to 127, as said below
- slot_rank: int32 [32768, 32], P(('expert', 'dp')), may hold values from -1 to 47, as said below
- image_id: int32 [32768], P(('expert', 'dp')), may hold values from 0 to 4095, as said below
- params: float32 [128, 848, 256], P('expert'), may hold values from -5 to 5
- first_moment: float32 [128, 848, 256], P('expert'), may hold values from -0.75 to 0.75
- second_moment: float32 [128, 848, 256], P('expert'), may hold values from 1e-06 to 0.01
- code_table: float32 [4096, 64], P(('expert', 'dp')), may hold values from -6 to 6
- table_first: float32 [4096, 64], P(('expert', 'dp')), may hold values from -0.75 to 0.75
- table_second: float32 [4096, 64], P(('expert', 'dp')), may hold values from 1e-06 to 0.01
Outputs:
- ray_loss: float32 [32768], P(('expert', 'dp'))
- new_params: float32 [128, 848, 256], P('expert')
- new_first_moment: float32 [128, 848, 256], P('expert')
- new_second_moment: float32 [128, 848, 256], P('expert')
- new_code_table: float32 [4096, 64], P(('expert', 'dp'))
- new_table_first: float32 [4096, 64], P(('expert', 'dp'))
- new_table_second: float32 [4096, 64], P(('expert', 'dp'))
Inputs may be any that keep to these rules, and one draw needn't show every extreme that they name: `ray_length`: rays form aligned blocks of 128, one a device, in the order of the axes expert then dp. In every block the lengths sum to 3072 and some ray has all 32 samples. `cell_id`: also given for samples at or beyond their ray's length, where it is unused. `slot_rank`: for a sample below its ray's length: its rank among the live samples of its block of 128 rays that have the same cell_id, counted ray by ray and along each ray; -1 for the other samples. No block has more than 48 live samples of one cell_id; in every block some cell_id has exactly 48, and one cell_id has 48 in every block. `image_id`: A ray of block b names an image from b * 16 to (b + 1) * 16 - 1.
All inputs are finite; a program needn't handle non-finite values.
Results may differ from a plain program's by a relative error of at most 0.0046.
Values may be sent and summed in bfloat16 or wider, within the bound.
No kernel may reach another device: no remote copies, remote signals or barrier semaphores. Data moves between devices by JAX's collectives and lax.ppermute only.
A program may use at most 128 MiB of HBM per device.

v0:
```python
import functools

import jax
import jax.numpy as jnp
from jax import lax
from jax.experimental import pallas as pl
from jax.experimental.pallas import tpu as pltpu
from jax.sharding import PartitionSpec as P

NET_WIDTH = 256
CODE_WIDTH = 64
ENC_WIDTH = 64
LAYERS = 4
SAMPLES = 32
RAYS = 128
IMAGES_DEV = 16
CAPACITY = 48
DEPTH = 16
THIRDS = CAPACITY // DEPTH
PARTS = 2
HEAD_ROW = ENC_WIDTH + (LAYERS - 1) * NET_WIDTH
PARAM_ROWS = HEAD_ROW + 16

F32 = jnp.float32
BF16 = jnp.bfloat16

BETA_ONE = 0.9
BETA_TWO = 0.999
LEARN_RATE = 0.001
ADAM_EPS = 1e-08
CORRECT_ONE = 1.0 - 0.9**10
CORRECT_TWO = 1.0 - 0.999**10

NN = (((1,), (0,)), ((), ()))
NT = (((1,), (1,)), ((), ()))
TN = (((0,), (0,)), ((), ()))


def mul(left, right, dims=NN):
    return lax.dot_general(left, right, dims, preferred_element_type=F32)


def iota(shape, dim):
    return lax.broadcasted_iota(jnp.int32, shape, dim)


def three_parts(value):
    high = value.astype(BF16)
    rest = value - high.astype(F32)
    middle = rest.astype(BF16)
    low = (rest - middle.astype(F32)).astype(BF16)
    return [high, middle, low]


def adam_update(param_now, gradient, moment_one, moment_two):
    new_one = BETA_ONE * moment_one + (1.0 - BETA_ONE) * gradient
    new_two = BETA_TWO * moment_two + (1.0 - BETA_TWO) * gradient * gradient
    update = LEARN_RATE * (new_one / CORRECT_ONE) / (jnp.sqrt(new_two / CORRECT_TWO) + ADAM_EPS)
    return (param_now - update, new_one, new_two)


def dispatch_kernel(
    feat_in, cell_in, rank_in, out_ref, hot_ref, rows_ref, feat_ref, cell_ref, rank_ref, sems
):
    places = out_ref.shape[0]
    moves = [
        pltpu.make_async_copy(source, target, sems.at[i])
        for i, (source, target) in enumerate(
            ((cell_in, cell_ref), (rank_in, rank_ref), (feat_in, feat_ref))
        )
    ]
    for move in moves:
        move.start()
    for move in moves:
        move.wait()
    for i in range(SAMPLES):
        cell = cell_ref[i : i + 1, :]
        rank = rank_ref[i : i + 1, :]
        place = jnp.where(rank >= 0, (cell >> 1) * DEPTH + (rank & (DEPTH - 1)), -1)
        inner = (rank >> 4) * 2 + (cell & 1)
        span = slice(i * RAYS, (i + 1) * RAYS)
        hot_ref[:, span] = jnp.where(iota((places, RAYS), 0) == place, 1.0, 0.0).astype(BF16)
        feat = feat_ref[i].astype(F32)
        for q in range(THIRDS * 2):
            rows_ref[q * ENC_WIDTH : (q + 1) * ENC_WIDTH, span] = jnp.where(
                inner == q, feat, 0.0
            ).astype(BF16)
    out_ref[...] = mul(hot_ref[...], rows_ref[...], NT).astype(BF16)


def depth_match(rows):
    return (iota((rows, 128), 0) & (DEPTH - 1)) == (iota((rows, 128), 1) & (DEPTH - 1))


def first_matrix(weights_ref, held):
    matrix = weights_ref[held, 0:ENC_WIDTH, :]
    blank = jnp.zeros_like(matrix)
    return jnp.concatenate([matrix, blank] if held == 0 else [blank, matrix], axis=0)


def hidden_matrix(weights_ref, held, layer):
    start = ENC_WIDTH + (layer - 1) * NET_WIDTH
    return weights_ref[held, start : start + NET_WIDTH, :]


def head_tile(head, held):
    rows = jnp.concatenate(
        [jnp.broadcast_to(head[c : c + 1, :], (DEPTH, NET_WIDTH)) for c in range(4)], axis=0
    )
    blank = jnp.zeros_like(rows)
    return jnp.concatenate([rows, blank] if held == 0 else [blank, rows], axis=0).astype(BF16)


def slot_rows(x_ref):
    return jnp.concatenate([x_ref[:, j * 128 : (j + 1) * 128] for j in range(THIRDS)], axis=0)


def forward_kernel(
    x_ref, params_ref, acts0_ref, acts1_ref, out_ref, weights_ref, lines_ref, held_ref, sems
):
    groups = out_ref.shape[0]
    rows = held_ref.shape[1]
    moves = []
    weights_ref[...] = params_ref[...].astype(BF16)
    heads = [weights_ref[h, HEAD_ROW:PARAM_ROWS, :].astype(F32) for h in range(2)]
    for j in range(4):
        h, c = j // 2, (j % 2) * 2
        pair = jnp.concatenate(
            [heads[h][4 + c : 5 + c, :CODE_WIDTH], heads[h][5 + c : 6 + c, :CODE_WIDTH]], axis=1
        )
        lines_ref[:, 3 + j, :] = jnp.broadcast_to(pair, (groups, 128))
    lane = iota((1, 128), 1)
    shift = jnp.zeros((1, 128), F32)
    total = jnp.zeros((rows, 128), F32)
    for h, acts_ref in enumerate((acts0_ref, acts1_ref)):
        current = slot_rows(x_ref)
        for k in range(LAYERS):
            matrix = first_matrix(weights_ref, h) if k == 0 else hidden_matrix(weights_ref, h, k)
            preact = mul(current, matrix) + heads[h][9 + k : 10 + k, :]
            current = jnp.maximum(preact, 0.0).astype(BF16)
            place = h * LAYERS + k
            held_ref[place] = current
            move = pltpu.make_async_copy(held_ref.at[place], acts_ref.at[k], sems.at[place])
            move.start()
            moves.append(move)
        total = total + mul(current, head_tile(heads[h], h), NT)
        for c in range(4):
            shift = shift + jnp.where((lane >> 4) == h * 4 + c, heads[h][8:9, c : c + 1], 0.0)
    total = jnp.where(depth_match(rows), total + shift, 0.0)
    raw = jnp.sum(total.reshape(THIRDS * groups, DEPTH, 128), axis=1)
    low = raw - raw.astype(BF16).astype(F32)
    density = []
    for j in range(THIRDS):
        span = slice(j * groups, (j + 1) * groups)
        lines_ref[:, j, :] = raw[span]
        density += [low[span, 0:DEPTH], low[span, 64 : 64 + DEPTH]]
    lines_ref[:, 7, :] = jnp.concatenate(density + [jnp.zeros((groups, 32), F32)], axis=1)
    out_ref[...] = lines_ref[...].astype(BF16)
    for move in moves:
        move.wait()


def one_sample_row(cell_ref, rank_ref, image, i, owners):
    cell = cell_ref[pl.ds(i, 1), :]
    rank = rank_ref[pl.ds(i, 1), :]
    live = rank >= 0
    owner = jnp.where(live, cell >> 1, -1)
    hot = jnp.where(iota((owners, RAYS), 0) == owner, 1.0, 0.0).astype(BF16)
    held = cell & 1
    slot = jnp.where(live, ((rank >> 4) * 2 + held) * DEPTH + (rank & (DEPTH - 1)), -1)
    code = jnp.where(live, held * IMAGES_DEV + image, -1)
    slot_mask = iota((THIRDS * 2 * DEPTH, RAYS), 0) == slot
    code_mask = iota((2 * IMAGES_DEV, RAYS), 0) == code
    masks = [slot_mask[q * DEPTH : (q + 1) * DEPTH] for q in range(THIRDS * 2)]
    masks += [code_mask[h * IMAGES_DEV : (h + 1) * IMAGES_DEV] for h in range(2)]
    return hot, masks


def running_sum(value):
    step = 1
    while step < SAMPLES:
        value = value + jnp.concatenate(
            [jnp.zeros((step, RAYS), F32), value[: SAMPLES - step]], axis=0
        )
        step *= 2
    return value


def running_sum_back(value):
    step = 1
    while step < SAMPLES:
        value = value + jnp.concatenate([value[step:], jnp.zeros((step, RAYS), F32)], axis=0)
        step *= 2
    return value


def ray_kernel(
    back_ref,
    cell_ref,
    rank_ref,
    image_ref,
    length_ref,
    spacing_ref,
    targets_ref,
    code_ref,
    first_ref,
    second_ref,
    out_ref,
    loss_ref,
    new_code_ref,
    new_first_ref,
    new_second_ref,
    table_ref,
    raw_ref,
    lines_ref,
):
    owners = back_ref.shape[0]
    image = image_ref[...] & (IMAGES_DEV - 1)
    code = code_ref[...].astype(BF16).astype(F32)
    tile = jnp.concatenate([code] * 8, axis=0)
    tile = jnp.concatenate([tile, tile], axis=1)
    block_row = iota((128, 128), 0) >> 4
    block_lane = iota((128, 128), 1) >> 6
    code_blocks = [
        jnp.where(block_row == 2 * j + block_lane, tile, 0.0).astype(BF16) for j in range(4)
    ]
    lines_ref[...] = back_ref[...].astype(F32)
    queries = [lines_ref[:, 3 + j, :].astype(BF16) for j in range(4)]
    code_part = mul(queries[0], code_blocks[0], NT)
    for j in range(1, 4):
        code_part = code_part + mul(queries[j], code_blocks[j], NT)
    code_parts = three_parts(code_part.T)
    lows = lines_ref[:, 7, :]
    blank = jnp.zeros((owners, 64 - DEPTH), F32)
    highs, rests = [], []
    for j in range(THIRDS):
        start = j * 2 * DEPTH
        rest = [lows[:, start : start + DEPTH], blank]
        rest += [lows[:, start + DEPTH : start + 2 * DEPTH], blank]
        highs.append(lines_ref[:, j, :].T.astype(BF16))
        rests.append(jnp.concatenate(rest, axis=1).T.astype(BF16))
    table_ref[...] = jnp.concatenate(
        [
            jnp.concatenate(highs + code_parts[0:1], axis=0),
            jnp.concatenate(rests + code_parts[1:2], axis=0),
        ],
        axis=1,
    )

    def pick(i, carry):
        sides = [one_sample_row(cell_ref, rank_ref, image, 2 * i + half, owners) for half in range(2)]
        hots = jnp.concatenate([side[0] for side in sides], axis=1)
        found = mul(table_ref[...], jnp.concatenate([hots] * PARTS, axis=0))
        for half in range(2):
            masks = sides[half][1]
            for c in range(4):
                total = jnp.zeros((DEPTH, RAYS), F32)
                for q in range(THIRDS * 2 + 2):
                    start = q * 64 + c * DEPTH
                    total = total + jnp.where(
                        masks[q], found[start : start + DEPTH, half * RAYS : (half + 1) * RAYS], 0.0
                    )
                raw_ref[c, pl.ds(2 * i + half, 1), :] = jnp.sum(total, axis=0, keepdims=True)
        return carry

    lax.fori_loop(0, SAMPLES // 2, pick, 0, unroll=4)

    spacing = spacing_ref[...]
    live = jnp.where(iota((SAMPLES, RAYS), 0) < length_ref[...], 1.0, 0.0)
    raw_density = raw_ref[0]
    small = jnp.exp(-jnp.abs(raw_density))
    density = jnp.maximum(raw_density, 0.0) + jnp.log1p(small)
    slope = jnp.where(raw_density >= 0, 1.0, small) / (1.0 + small)
    colors = []
    for c in range(3):
        raw_color = raw_ref[1 + c]
        tail = jnp.exp(-jnp.abs(raw_color))
        colors.append(jnp.where(raw_color >= 0, 1.0, tail) / (1.0 + tail))
    reach = spacing * live
    tau = density * reach
    before = running_sum(tau) - tau
    passed = jnp.exp(-before)
    kept = jnp.exp(-tau)
    weight = passed * (1.0 - kept)
    gaps = []
    loss = jnp.zeros((1, RAYS), F32)
    for c in range(3):
        gap = jnp.sum(weight * colors[c], axis=0, keepdims=True) - targets_ref[c : c + 1, :]
        gaps.append(gap)
        loss = loss + gap * gap
    loss_ref[...] = 0.5 * loss
    pull = gaps[0] * colors[0] + gaps[1] * colors[1] + gaps[2] * colors[2]
    behind = weight * pull
    tau_grad = pull * passed * kept - (running_sum_back(behind) - behind)
    raw_ref[0] = (tau_grad * reach * slope).astype(BF16).astype(F32)
    for c in range(3):
        raw_ref[1 + c] = (
            (weight * gaps[c] * (colors[c] * (1.0 - colors[c]))).astype(BF16).astype(F32)
        )

    def put(i, total):
        hots, rows = [], []
        for half in range(2):
            hot, masks = one_sample_row(cell_ref, rank_ref, image, 2 * i + half, owners)
            cots = [raw_ref[c, pl.ds(2 * i + half, 1), :] for c in range(4)]
            hots.append(hot)
            rows.append(
                jnp.concatenate(
                    [
                        jnp.where(masks[q], cots[c], 0.0)
                        for q in range(THIRDS * 2 + 2)
                        for c in range(4)
                    ],
                    axis=0,
                ).astype(BF16)
            )
        return total + mul(
            jnp.concatenate(rows, axis=1), jnp.concatenate(hots, axis=1), NT
        )

    placed = lax.fori_loop(
        0, SAMPLES // 2, put, jnp.zeros((512, owners), F32), unroll=4
    )
    for j in range(THIRDS):
        lines_ref[:, j, :] = placed[j * 128 : (j + 1) * 128].T
    image_sums = placed[384:512]
    sums_parts = three_parts(image_sums)
    sums_wide = jnp.concatenate(sums_parts, axis=1)
    sums_flip = jnp.concatenate(three_parts(image_sums.T), axis=1)
    table_grad = jnp.zeros((IMAGES_DEV, CODE_WIDTH), F32)
    for j in range(4):
        lines_ref[:, 3 + j, :] = mul(sums_flip, jnp.concatenate([code_blocks[j]] * 3, axis=0))
        product = mul(sums_wide, jnp.concatenate([queries[j]] * 3, axis=0))
        low = 2 * j * IMAGES_DEV
        table_grad = table_grad + product[low : low + IMAGES_DEV, :CODE_WIDTH]
        table_grad = table_grad + product[low + IMAGES_DEV : low + 2 * IMAGES_DEV, CODE_WIDTH:]
    lines_ref[:, 7, :] = jnp.zeros((owners, 128), F32)
    out_ref[...] = lines_ref[...].astype(BF16)
    new_code, new_first, new_second = adam_update(
        code_ref[...], table_grad, first_ref[...], second_ref[...]
    )
    new_code_ref[...] = new_code
    new_first_ref[...] = new_first
    new_second_ref[...] = new_second


def backward_kernel(
    h,
    order_ref,
    x_ref,
    acts_ref,
    cot_in_ref,
    weights_ref,
    own_ref,
    first_ref,
    second_ref,
    third_ref,
    total_ref,
    cot_ref,
):
    third = pl.program_id(0)
    groups = cot_ref.shape[0]
    rows = x_ref.shape[0]

    @pl.when(third == 0)
    def _():
        cot_ref[...] = cot_in_ref[...].astype(F32)
        total_ref[...] = jnp.zeros_like(total_ref)
        lines = []
        for c in range(4):
            sums = jnp.sum(cot_ref[:, 3 + h * 2 + c // 2, :], axis=0, keepdims=True)
            start = (c % 2) * CODE_WIDTH
            line = sums[:, start : start + CODE_WIDTH]
            lines.append(
                jnp.concatenate([line, jnp.zeros((1, NET_WIDTH - CODE_WIDTH), F32)], axis=1)
            )
        total_ref[HEAD_ROW:PARAM_ROWS, :] = jnp.concatenate(
            [jnp.zeros((4, NET_WIDTH), F32)] + lines + [jnp.zeros((8, NET_WIDTH), F32)], axis=0
        )

    cot = jnp.where(
        third == 0, cot_ref[:, 0, :], jnp.where(third == 1, cot_ref[:, 1, :], cot_ref[:, 2, :])
    )
    sums = jnp.sum(cot, axis=0, keepdims=True)
    spread = jnp.broadcast_to(cot[:, None, :], (groups, DEPTH, 128)).reshape(rows, 128)
    spread = jnp.where(depth_match(rows), spread, 0.0).astype(BF16)
    lane = iota((1, 128), 1)
    wide_lane = iota((1, NET_WIDTH), 1)
    head = weights_ref[0, HEAD_ROW:PARAM_ROWS, :].astype(F32)
    outer = mul(spread, acts_ref[LAYERS - 1], TN)[h * 64 : (h + 1) * 64]
    head_grad = jnp.sum(outer.reshape(4, DEPTH, NET_WIDTH), axis=1)
    bias_head = jnp.zeros((1, NET_WIDTH), F32)
    for c in range(4):
        value = jnp.sum(jnp.where((lane >> 4) == h * 4 + c, sums, 0.0), axis=1, keepdims=True)
        bias_head = bias_head + jnp.where(wide_lane == c, value, 0.0)
    up = mul(spread, head_tile(head, h))
    bias_lines = [None] * LAYERS
    for k in reversed(range(LAYERS)):
        pre_grad = jnp.where(acts_ref[k].astype(F32) > 0, up, 0.0).astype(BF16)
        bias_lines[k] = jnp.sum(pre_grad.astype(F32), axis=0, keepdims=True)
        if k > 0:
            start = ENC_WIDTH + (k - 1) * NET_WIDTH
            total_ref[start : start + NET_WIDTH, :] += mul(acts_ref[k - 1], pre_grad, TN)
            up = mul(pre_grad, weights_ref[0, start : start + NET_WIDTH, :], NT)
        else:
            total_ref[0:ENC_WIDTH, :] += mul(x_ref[...], pre_grad, TN)[
                h * ENC_WIDTH : (h + 1) * ENC_WIDTH
            ]
    total_ref[HEAD_ROW:PARAM_ROWS, :] += jnp.concatenate(
        [head_grad, jnp.zeros((4, NET_WIDTH), F32), bias_head]
        + bias_lines
        + [jnp.zeros((3, NET_WIDTH), F32)],
        axis=0,
    )

    @pl.when(third == THIRDS - 1)
    def _():
        quarter = own_ref.shape[0]
        for k, share_ref in enumerate((own_ref, first_ref, second_ref, third_ref)):
            start = pl.multiple_of(order_ref[k] * quarter, 8)
            share_ref[...] = total_ref[pl.ds(start, quarter), :].astype(share_ref.dtype)


def adam_kernel(
    order_ref,
    own_ref,
    first_ref,
    second_ref,
    third_ref,
    param_ref,
    one_ref,
    two_ref,
    *refs,
):
    step = pl.program_id(0)
    new_param_ref, new_one_ref, new_two_ref = refs[-3:]
    for k, share_ref in enumerate((own_ref, first_ref, second_ref, third_ref)):

        @pl.when(step == k)
        def _():
            new_param, new_one, new_two = adam_update(
                param_ref[0], share_ref[...].astype(F32), one_ref[0], two_ref[0]
            )
            new_param_ref[0] = new_param
            new_one_ref[0] = new_one
            new_two_ref[0] = new_two


def cost(micros):
    return pl.CostEstimate(
        flops=int(micros * 1e9), bytes_accessed=int(micros * 3e6), transcendentals=0
    )


def limits(mib=48):
    return pltpu.CompilerParams(vmem_limit_bytes=mib * 1024 * 1024)


def shape_of(dims, kind):
    return jax.ShapeDtypeStruct(dims, kind)


def shards(
    features,
    spacing,
    targets,
    ray_length,
    cell_id,
    slot_rank,
    image_id,
    params,
    first_moment,
    second_moment,
    code_table,
    table_first,
    table_second,
):
    groups = lax.axis_size("expert")
    places = groups * DEPTH
    cell_rows = cell_id.T
    rank_rows = slot_rank.T
    outgoing = pl.pallas_call(
        dispatch_kernel,
        out_shape=shape_of((places, THIRDS * 128), BF16),
        in_specs=[pl.BlockSpec(memory_space=pl.ANY)] * 3,
        scratch_shapes=[
            pltpu.VMEM((places, SAMPLES * RAYS), BF16),
            pltpu.VMEM((THIRDS * 128, SAMPLES * RAYS), BF16),
            pltpu.VMEM((SAMPLES, ENC_WIDTH, RAYS), BF16),
            pltpu.VMEM((SAMPLES, RAYS), jnp.int32),
            pltpu.VMEM((SAMPLES, RAYS), jnp.int32),
            pltpu.SemaphoreType.DMA((3,)),
        ],
        compiler_params=limits(59),
        name="dispatch",
    )(jnp.transpose(features, (1, 2, 0)), cell_rows, rank_rows)
    arrived = lax.all_to_all(outgoing, "expert", split_axis=0, concat_axis=0, tiled=True)

    slots = THIRDS * places
    vmem = pl.BlockSpec(memory_space=pltpu.VMEM)
    anywhere = pl.BlockSpec(memory_space=pl.ANY)
    acts_shape = shape_of((LAYERS, slots, NET_WIDTH), BF16)
    *acts, raw_out, weights = pl.pallas_call(
        forward_kernel,
        out_shape=[
            acts_shape,
            acts_shape,
            shape_of((groups, 8, 128), BF16),
            shape_of((2, PARAM_ROWS, NET_WIDTH), BF16),
        ],
        out_specs=[anywhere, anywhere, vmem, vmem],
        scratch_shapes=[
            pltpu.VMEM((groups, 8, 128), F32),
            pltpu.VMEM((2 * LAYERS, slots, NET_WIDTH), BF16),
            pltpu.SemaphoreType.DMA((2 * LAYERS,)),
        ],
        compiler_params=limits(48),
        name="forward",
    )(arrived, params)
    returned = lax.all_to_all(raw_out, "expert", split_axis=0, concat_axis=0, tiled=True)

    table_shape = shape_of(code_table.shape, F32)
    cot_out, loss, new_table, new_table_first, new_table_second = pl.pallas_call(
        ray_kernel,
        out_shape=[
            shape_of((groups, 8, 128), BF16),
            shape_of((1, RAYS), F32),
            table_shape,
            table_shape,
            table_shape,
        ],
        scratch_shapes=[
            pltpu.VMEM((512, PARTS * groups), BF16),
            pltpu.VMEM((4, SAMPLES, RAYS), F32),
            pltpu.VMEM((groups, 8, 128), F32),
        ],
        compiler_params=limits(16),
        name="rays",
    )(
        returned,
        cell_rows,
        rank_rows,
        image_id.reshape(1, RAYS),
        ray_length.reshape(1, RAYS),
        spacing.T,
        targets,
        code_table,
        table_first,
        table_second,
    )
    cot_in = lax.all_to_all(cot_out, "expert", split_axis=0, concat_axis=0, tiled=True)

    copies = lax.axis_size("dp")
    quarter = -(-PARAM_ROWS // (8 * copies)) * 8
    turns = jnp.arange(copies, dtype=jnp.int32)
    position = lax.axis_index("dp")
    lent = lambda *dims: pl.BlockSpec(dims, lambda i, order: (0,) * len(dims))

    def send(value, distance):
        return lax.ppermute(value, "dp", [(i, (i + distance) % copies) for i in range(copies)])

    def gradient(h):
        return pl.pallas_call(
            functools.partial(backward_kernel, h),
            grid_spec=pltpu.PrefetchScalarGridSpec(
                num_scalar_prefetch=1,
                grid=(THIRDS,),
                in_specs=[
                    pl.BlockSpec((places, 128), lambda i, order: (0, i)),
                    pl.BlockSpec((LAYERS, places, NET_WIDTH), lambda i, order: (0, i, 0)),
                    lent(groups, 8, 128),
                    pl.BlockSpec((1, PARAM_ROWS, NET_WIDTH), lambda i, order: (h, 0, 0)),
                ],
                out_specs=[lent(quarter, NET_WIDTH)] * 4,
                scratch_shapes=[
                    pltpu.VMEM((copies * quarter, NET_WIDTH), F32),
                    pltpu.VMEM((groups, 8, 128), F32),
                ],
            ),
            out_shape=[shape_of((quarter, NET_WIDTH), F32)]
            + [shape_of((quarter, NET_WIDTH), BF16)] * 3,
            compiler_params=limits(48),
            cost_estimate=cost(6.0),
            name="backward",
        )((position + turns) % copies, arrived, acts[h], cot_in, weights)

    def collect(shares):
        share = shares[0]
        for k in (2, 1, 3):
            share = share + send(shares[k], k).astype(F32)
        share = share.astype(BF16)
        behind, ahead = send(share, 1), send(share, 3)
        return share, behind, send(ahead, 3), ahead

    def update(h, pieces, earlier):
        block = pl.BlockSpec((1, quarter, NET_WIDTH), lambda i, order: (h, order[i], 0))
        return pl.pallas_call(
            adam_kernel,
            grid_spec=pltpu.PrefetchScalarGridSpec(
                num_scalar_prefetch=1,
                grid=(copies,),
                in_specs=[lent(quarter, NET_WIDTH)] * 4
                + [block] * 3
                + [pl.BlockSpec(memory_space=pl.ANY)] * len(earlier),
                out_specs=[block] * 3,
            ),
            out_shape=[shape_of(params.shape, F32)] * 3,
            input_output_aliases={8 + i: i for i in range(len(earlier))},
            compiler_params=limits(12),
            cost_estimate=cost(2.0),
            name="adam",
        )(
            (position - turns) % copies,
            *pieces,
            params,
            first_moment,
            second_moment,
            *earlier,
        )

    pieces = [collect(gradient(h)) for h in range(2)]
    updated = update(0, pieces[0], ())
    new_params, new_first, new_second = update(1, pieces[1], updated)
    return (
        loss.reshape(RAYS),
        new_params,
        new_first,
        new_second,
        new_table,
        new_table_first,
        new_table_second,
    )


def solution(mesh):
    rays = ("expert", "dp")
    table = P(rays, None)
    block = P("expert", None, None)
    return jax.shard_map(
        shards,
        mesh=mesh,
        in_specs=(
            P(rays, None, None),
            P(rays, None),
            P(None, rays),
            P(rays),
            P(rays, None),
            P(rays, None),
            P(rays),
            block,
            block,
            block,
            table,
            table,
            table,
        ),
        out_specs=(P(rays), block, block, block, table, table, table),
        check_vma=False,
    )
```

profile of v0, /device:TPU:2, one launch (start us, length us, event | category | flops | bytes accessed | tf_op | source)
XLA Modules:
  0.0 128.6 jit_solution(12328380973844653352)
XLA Ops:
  0.6 0.0 copy-start
  0.6 7.2 %dispatch.1 = bf16[1024,384]{1,0:T(8,128)(2,1)} custom-call(bf16[32,64,128]{2,1,0:T(8,128)(2,1)} %bitcast.20, s32[32,128]{1,0:T(8,128)} %bitcast.12, s32[32,128]{1,0:T(8,128)} %bitcast.14), custom_call_target="tpu_custom_call" | custom-call | tf_op jit(solution)/shard_map/dispatch/pallas_call | solution.py:482
  7.9 35.2 %all_to_all.21 = bf16[64,16,384]{2,1,0:T(8,128)(2,1)S(1)} all-to-all(bf16[64,16,384]{2,1,0:T(8,128)(2,1)} %bitcast.19), channel_id=1, replica_groups=mesh['expert'=64,'dp'=4] {'expert'}, dimensions={0} | all-to-all | bytes 1572864 | tf_op jit(solution)/shard_map/all_to_all | solution.py:497
  43.1 0.0 copy-start.7
  43.1 0.0 copy-start.8
  43.1 0.0 copy-start.9
  43.1 0.0 copy-start.10
  43.1 0.0 copy-start.11
  43.1 0.0 copy-done
  43.1 5.5 %forward.1 = (bf16[4,3072,256]{2,1,0:T(8,128)(2,1)}, bf16[4,3072,256]{2,1,0:T(8,128)(2,1)}, bf16[64,8,128]{2,1,0:T(8,128)(2,1)S(1)}, bf16[2,848,256]{2,1,0:T(8,128)(2,1)S(1)}) custom-call(bf16[1024,384]{1,0:T(8,128)(2,1)S(1)} %bitcast.9, f32[2,848,256]{2,1,0:T(8,128)S(1)} %copy-done), custom_call_target="tpu_custom_call" | custom-call | tf_op jit(solution)/shard_map/forward/pallas_call | solution.py:503
  48.7 15.6 %all_to_all.22.back_ref = bf16[64,8,128]{2,1,0:T(8,128)(2,1)S(1)} all-to-all(bf16[64,8,128]{2,1,0:T(8,128)(2,1)S(1)} %get-tuple-element.30), channel_id=1, replica_groups=mesh['expert'=64,'dp'=4] {'expert'}, dimensions={0} | all-to-all | bytes 262144 | tf_op jit(solution)/shard_map/all_to_all | solution.py:520
  64.3 0.0 copy-done.3
  64.3 0.0 copy-done.4
  64.3 0.0 copy-done.5
  64.3 0.0 copy-done.6
  64.3 5.4 %rays.1 = (bf16[64,8,128]{2,1,0:T(8,128)(2,1)}, f32[1,128]{1,0:T(1,128)}, f32[16,64]{1,0:T(8,128)}, f32[16,64]{1,0:T(8,128)}, f32[16,64]{1,0:T(8,128)}) custom-call(bf16[64,8,128]{2,1,0:T(8,128)(2,1)S(1)} %all_to_all.22.back_ref, s32[32,128]{1,0:T(8,128)S(1)} %bitcast.13, s32[32,128]{1,0:T(8,128)S(1)} %bitcast.15, s32[1,128]{1,0:T(1,128)S(1)} %bitcast.17, ...), custom_call_target="tpu_custom_call" | custom-call | tf_op jit(solution)/shard_map/rays/pallas_call | solution.py:523
  69.7 5.6 %all-to-all-start.2 = ((bf16[64,8,128]{2,1,0:T(8,128)(2,1)}), bf16[64,8,128]{2,1,0:T(8,128)(2,1)S(1)}, u32[]{:S(2)}, u32[]{:S(2)}) async-start(bf16[64,8,128]{2,1,0:T(8,128)(2,1)} %get-tuple-element.33), calls=%async_computation.2 | async-start | bytes 262144 | tf_op jit(solution)/shard_map/all_to_all | solution.py:551
  75.4 10.0 %all-to-all-done.2.cot_in_ref = bf16[64,8,128]{2,1,0:T(8,128)(2,1)S(1)} async-done(((bf16[64,8,128]{2,1,0:T(8,128)(2,1)}), bf16[64,8,128]{2,1,0:T(8,128)(2,1)S(1)}, u32[]{:S(2)}, u32[]{:S(2)}) %all-to-all-start.2) | async-done | bytes 131104 | tf_op jit(solution)/shard_map/all_to_all | solution.py:551
  85.4 7.1 %backward.3 = (f32[216,256]{1,0:T(8,128)S(1)}, bf16[216,256]{1,0:T(8,128)(2,1)S(1)}, bf16[216,256]{1,0:T(8,128)(2,1)S(1)}, bf16[216,256]{1,0:T(8,128)(2,1)S(1)}) custom-call(s32[4]{0:T(128)S(1)} %and_select_fusion.order_ref, bf16[1024,384]{1,0:T(8,128)(2,1)S(1)} %bitcast.10, bf16[4,3072,256]{2,1,0:T(8,128)(2,1)} %get-tuple-element.39.acts_ref, ...), custom_call_target="tpu_custom_call" | custom-call | flops 6000000000 | bytes 18000000 | tf_op jit(solution)/shard_map/backward/pallas_call | solution.py:563
  92.4 3.3 %collective-permute-start.6 = (bf16[216,256]{1,0:T(8,128)(2,1)S(1)}, bf16[216,256]{1,0:T(8,128)(2,1)S(1)}, u32[]{:S(2)}, u32[]{:S(2)}) collective-permute-start(bf16[216,256]{1,0:T(8,128)(2,1)S(1)} %get-tuple-element.41), channel_id=1, source_target_pairs={{0,2},{1,3},{2,0},{3,1},{4,6},{5,7},{6,4},{7,5},{8,10},{9,11},{10,... | collective-permute-start | bytes 331784 | tf_op jit(solution)/shard_map/ppermute | solution.py:560
  95.7 0.7 collective-permute-start.7
  96.4 2.6 %collective-permute-start.8 = (bf16[216,256]{1,0:T(8,128)(2,1)S(1)}, bf16[216,256]{1,0:T(8,128)(2,1)S(1)}, u32[]{:S(2)}, u32[]{:S(2)}) collective-permute-start(bf16[216,256]{1,0:T(8,128)(2,1)S(1)} %get-tuple-element.43), channel_id=1, source_target_pairs={{0,3},{1,0},{2,1},{3,2},{4,7},{5,4},{6,5},{7,6},{8,11},{9,8},{10,9... | collective-permute-start | bytes 331784 | tf_op jit(solution)/shard_map/ppermute | solution.py:560
  98.9 7.4 %backward.2 = (f32[216,256]{1,0:T(8,128)S(1)}, bf16[216,256]{1,0:T(8,128)(2,1)S(1)}, bf16[216,256]{1,0:T(8,128)(2,1)S(1)}, bf16[216,256]{1,0:T(8,128)(2,1)S(1)}) custom-call(s32[4]{0:T(128)S(1)} %and_select_fusion.order_ref, bf16[1024,384]{1,0:T(8,128)(2,1)S(1)} %bitcast.11, bf16[4,3072,256]{2,1,0:T(8,128)(2,1)} %get-tuple-element.32.acts_ref, ...), custom_call_target="tpu_custom_call" | custom-call | flops 6000000000 | bytes 18000000 | tf_op jit(solution)/shard_map/backward/pallas_call | solution.py:563
  106.3 0.1 collective-permute-start
  106.4 0.8 collective-permute-start.1
  107.3 0.0 collective-permute-done.6
  107.3 2.5 %collective-permute-start.2 = (bf16[216,256]{1,0:T(8,128)(2,1)S(1)}, bf16[216,256]{1,0:T(8,128)(2,1)S(1)}, u32[]{:S(2)}, u32[]{:S(2)}) collective-permute-start(bf16[216,256]{1,0:T(8,128)(2,1)S(1)} %get-tuple-element.38), channel_id=1, source_target_pairs={{0,3},{1,0},{2,1},{3,2},{4,7},{5,4},{6,5},{7,6},{8,11},{9,8},{10,9... | collective-permute-start | bytes 331784 | tf_op jit(solution)/shard_map/ppermute | solution.py:560
  109.7 0.0 collective-permute-done.7
  109.7 0.0 collective-permute-done.8
  109.7 0.1 add_convert_fusion.own_ref
  109.8 0.9 collective-permute-start.10
  110.7 1.2 collective-permute-start.9
  111.9 1.9 %collective-permute-done = bf16[216,256]{1,0:T(8,128)(2,1)S(1)} collective-permute-done((bf16[216,256]{1,0:T(8,128)(2,1)S(1)}, bf16[216,256]{1,0:T(8,128)(2,1)S(1)}, u32[]{:S(2)}, u32[]{:S(2)}) %collective-permute-start) | collective-permute-done | bytes 110624 | tf_op jit(solution)/shard_map/ppermute | solution.py:560
  113.8 1.1 collective-permute-done.1
  114.9 0.0 collective-permute-done.2
  114.9 0.1 add_convert_fusion.1.own_ref
  115.0 1.8 %collective-permute-start.4 = (bf16[216,256]{1,0:T(8,128)(2,1)S(1)}, bf16[216,256]{1,0:T(8,128)(2,1)S(1)}, u32[]{:S(2)}, u32[]{:S(2)}) collective-permute-start(bf16[216,256]{1,0:T(8,128)(2,1)S(1)} %add_convert_fusion.1.own_ref), channel_id=1, source_target_pairs={{0,3},{1,0},{2,1},{3,2},{4,7},{5,4},{6,5},{7,6},{8,11},{9,8},{10,9... | collective-permute-start | bytes 331784 | tf_op jit(solution)/shard_map/ppermute | solution.py:560
  116.8 0.0 collective-permute-done.10.third_ref
  116.8 0.8 collective-permute-start.11
  117.6 1.2 collective-permute-start.3
  118.8 1.4 %collective-permute-done.4.third_ref = bf16[216,256]{1,0:T(8,128)(2,1)S(1)} collective-permute-done((bf16[216,256]{1,0:T(8,128)(2,1)S(1)}, bf16[216,256]{1,0:T(8,128)(2,1)S(1)}, u32[]{:S(2)}, u32[]{:S(2)}) %collective-permute-start.4) | collective-permute-done | bytes 110624 | tf_op jit(solution)/shard_map/ppermute | solution.py:560
  120.2 2.5 %collective-permute-start.5 = (bf16[216,256]{1,0:T(8,128)(2,1)S(1)}, bf16[216,256]{1,0:T(8,128)(2,1)S(1)}, u32[]{:S(2)}, u32[]{:S(2)}) collective-permute-start(bf16[216,256]{1,0:T(8,128)(2,1)S(1)} %collective-permute-done.4.third_ref), channel_id=1, source_target_pairs={{0,3},{1,0},{2,1},{3,2},{4,7},{5,4},{6,5},{7,6},{8,11},{9,8},{10,9... | collective-permute-start | bytes 331784 | tf_op jit(solution)/shard_map/ppermute | solution.py:560
  122.8 0.0 collective-permute-done.9.first_ref
  122.8 0.0 collective-permute-done.11.second_ref
  122.8 2.9 %adam.2 = (f32[2,848,256]{2,1,0:T(8,128)}, f32[2,848,256]{2,1,0:T(8,128)}, f32[2,848,256]{2,1,0:T(8,128)}) custom-call(s32[4]{0:T(128)S(1)} %and_select_fusion.1.order_ref, bf16[216,256]{1,0:T(8,128)(2,1)S(1)} %add_convert_fusion.own_ref, bf16[216,256]{1,0:T(8,128)(2,1)S(1)} %collective-permute-done.9.first_ref, ...), custom_call_target="tpu_custom_call" | custom-call | flops 2000000000 | bytes 6000000 | tf_op jit(solution)/shard_map/adam/pallas_call | solution.py:597
  125.7 0.0 collective-permute-done.3.first_ref
  125.7 0.0 collective-permute-done.5.second_ref
  125.7 2.9 %adam.3 = (f32[2,848,256]{2,1,0:T(8,128)}, f32[2,848,256]{2,1,0:T(8,128)}, f32[2,848,256]{2,1,0:T(8,128)}) custom-call(s32[4]{0:T(128)S(1)} %and_select_fusion.1.order_ref, bf16[216,256]{1,0:T(8,128)(2,1)S(1)} %add_convert_fusion.1.own_ref, ...), custom_call_target="tpu_custom_call", output_to_operand_aliasing={{0}: (8, {}), {1}: (9, {}), {2}: (10, {})} | custom-call | flops 2000000000 | bytes 6000000 | tf_op jit(solution)/shard_map/adam/pallas_call | solution.py:597
  (15 shorter events, 0.0 us)
Async XLA Ops:
  0.6 42.5 %copy-start = (f32[2,848,256]{2,1,0:T(8,128)S(1)}, f32[2,848,256]{2,1,0:T(8,128)}, u32[]{:S(2)}) copy-start(f32[2,848,256]{2,1,0:T(8,128)} %param_ref.3) | copy-start | bytes 5210116
  43.1 21.2 %copy-start.3 = (s32[128,32]{0,1:T(8,128)S(1)}, s32[128,32]{0,1:T(8,128)}, u32[]{:S(2)}) copy-start(s32[128,32]{0,1:T(8,128)} %param.17) | copy-start | bytes 49156
  43.1 21.2 %copy-start.4 = (s32[128,32]{0,1:T(8,128)S(1)}, s32[128,32]{0,1:T(8,128)}, u32[]{:S(2)}) copy-start(s32[128,32]{0,1:T(8,128)} %param.18) | copy-start | bytes 49156
  43.1 21.2 %copy-start.5 = (f32[128,32]{0,1:T(8,128)S(1)}, f32[128,32]{0,1:T(8,128)}, u32[]{:S(2)}) copy-start(f32[128,32]{0,1:T(8,128)} %param.14) | copy-start | bytes 49156
  43.1 21.2 %copy-start.6 = (f32[16,64]{1,0:T(8,128)S(1)}, f32[16,64]{1,0:T(8,128)}, u32[]{:S(2)}) copy-start(f32[16,64]{1,0:T(8,128)} %code_ref.1) | copy-start | bytes 12292
  43.1 21.2 %copy-start.7 = (f32[16,64]{1,0:T(8,128)S(1)}, f32[16,64]{1,0:T(8,128)}, u32[]{:S(2)}) copy-start(f32[16,64]{1,0:T(8,128)} %first_ref.1) | copy-start | bytes 12292
  43.1 21.2 %copy-start.8 = (f32[16,64]{1,0:T(8,128)S(1)}, f32[16,64]{1,0:T(8,128)}, u32[]{:S(2)}) copy-start(f32[16,64]{1,0:T(8,128)} %second_ref.1) | copy-start | bytes 12292
  43.1 21.2 %copy-start.9 = (f32[3,128]{1,0:T(4,128)S(1)}, f32[3,128]{1,0:T(4,128)}, u32[]{:S(2)}) copy-start(f32[3,128]{1,0:T(4,128)} %targets_ref.1) | copy-start | bytes 4612
  43.1 21.2 %copy-start.10 = (s32[128]{0:T(128)S(1)}, s32[128]{0:T(128)}, u32[]{:S(2)}) copy-start(s32[128]{0:T(128)} %param.19) | copy-start | bytes 1540
  43.1 21.2 %copy-start.11 = (s32[128]{0:T(128)S(1)}, s32[128]{0:T(128)}, u32[]{:S(2)}) copy-start(s32[128]{0:T(128)} %param.16) | copy-start | bytes 1540
  69.7 15.6 %all-to-all-start.2 = ((bf16[64,8,128]{2,1,0:T(8,128)(2,1)}), bf16[64,8,128]{2,1,0:T(8,128)(2,1)S(1)}, u32[]{:S(2)}, u32[]{:S(2)}) async-start(bf16[64,8,128]{2,1,0:T(8,128)(2,1)} %get-tuple-element.33), calls=%async_computation.2 | async-start | bytes 262144 | tf_op jit(solution)/shard_map/all_to_all | solution.py:551
  92.4 14.8 %collective-permute-start.6 = (bf16[216,256]{1,0:T(8,128)(2,1)S(1)}, bf16[216,256]{1,0:T(8,128)(2,1)S(1)}, u32[]{:S(2)}, u32[]{:S(2)}) collective-permute-start(bf16[216,256]{1,0:T(8,128)(2,1)S(1)} %get-tuple-element.41), channel_id=1, source_target_pairs={{0,2},{1,3},{2,0},{3,1},{4,6},{5,7},{6,4},{7,5},{8,10},{9,11},{10,... | collective-permute-start | bytes 331784 | tf_op jit(solution)/shard_map/ppermute | solution.py:560
  95.7 14.0 %collective-permute-start.7 = (bf16[216,256]{1,0:T(8,128)(2,1)S(1)}, bf16[216,256]{1,0:T(8,128)(2,1)S(1)}, u32[]{:S(2)}, u32[]{:S(2)}) collective-permute-start(bf16[216,256]{1,0:T(8,128)(2,1)S(1)} %get-tuple-element.42), channel_id=1, source_target_pairs={{0,1},{1,2},{2,3},{3,0},{4,5},{5,6},{6,7},{7,4},{8,9},{9,10},{10,1... | collective-permute-start | bytes 331784 | tf_op jit(solution)/shard_map/ppermute | solution.py:560
  96.4 13.4 %collective-permute-start.8 = (bf16[216,256]{1,0:T(8,128)(2,1)S(1)}, bf16[216,256]{1,0:T(8,128)(2,1)S(1)}, u32[]{:S(2)}, u32[]{:S(2)}) collective-permute-start(bf16[216,256]{1,0:T(8,128)(2,1)S(1)} %get-tuple-element.43), channel_id=1, source_target_pairs={{0,3},{1,0},{2,1},{3,2},{4,7},{5,4},{6,5},{7,6},{8,11},{9,8},{10,9... | collective-permute-start | bytes 331784 | tf_op jit(solution)/shard_map/ppermute | solution.py:560
  98.9 23.8 %copy-start.1 = (f32[2,848,256]{2,1,0:T(8,128)S(1)}, f32[2,848,256]{2,1,0:T(8,128)}, u32[]{:S(2)}) copy-start(f32[2,848,256]{2,1,0:T(8,128)} %one_ref.3) | copy-start | bytes 5210116
  98.9 23.8 %copy-start.2 = (f32[2,848,256]{2,1,0:T(8,128)S(1)}, f32[2,848,256]{2,1,0:T(8,128)}, u32[]{:S(2)}) copy-start(f32[2,848,256]{2,1,0:T(8,128)} %two_ref.3) | copy-start | bytes 5210116
  106.3 7.5 %collective-permute-start = (bf16[216,256]{1,0:T(8,128)(2,1)S(1)}, bf16[216,256]{1,0:T(8,128)(2,1)S(1)}, u32[]{:S(2)}, u32[]{:S(2)}) collective-permute-start(bf16[216,256]{1,0:T(8,128)(2,1)S(1)} %get-tuple-element.36), channel_id=1, source_target_pairs={{0,2},{1,3},{2,0},{3,1},{4,6},{5,7},{6,4},{7,5},{8,10},{9,11},{10,... | collective-permute-start | bytes 331784 | tf_op jit(solution)/shard_map/ppermute | solution.py:560
  106.4 8.5 %collective-permute-start.1 = (bf16[216,256]{1,0:T(8,128)(2,1)S(1)}, bf16[216,256]{1,0:T(8,128)(2,1)S(1)}, u32[]{:S(2)}, u32[]{:S(2)}) collective-permute-start(bf16[216,256]{1,0:T(8,128)(2,1)S(1)} %get-tuple-element.37), channel_id=1, source_target_pairs={{0,1},{1,2},{2,3},{3,0},{4,5},{5,6},{6,7},{7,4},{8,9},{9,10},{10,1... | collective-permute-start | bytes 331784 | tf_op jit(solution)/shard_map/ppermute | solution.py:560
  107.3 7.6 %collective-permute-start.2 = (bf16[216,256]{1,0:T(8,128)(2,1)S(1)}, bf16[216,256]{1,0:T(8,128)(2,1)S(1)}, u32[]{:S(2)}, u32[]{:S(2)}) collective-permute-start(bf16[216,256]{1,0:T(8,128)(2,1)S(1)} %get-tuple-element.38), channel_id=1, source_target_pairs={{0,3},{1,0},{2,1},{3,2},{4,7},{5,4},{6,5},{7,6},{8,11},{9,8},{10,9... | collective-permute-start | bytes 331784 | tf_op jit(solution)/shard_map/ppermute | solution.py:560
  109.8 7.0 %collective-permute-start.10 = (bf16[216,256]{1,0:T(8,128)(2,1)S(1)}, bf16[216,256]{1,0:T(8,128)(2,1)S(1)}, u32[]{:S(2)}, u32[]{:S(2)}) collective-permute-start(bf16[216,256]{1,0:T(8,128)(2,1)S(1)} %add_convert_fusion.own_ref), channel_id=1, source_target_pairs={{0,3},{1,0},{2,1},{3,2},{4,7},{5,4},{6,5},{7,6},{8,11},{9,8},{10,9... | collective-permute-start | bytes 331784 | tf_op jit(solution)/shard_map/ppermute | solution.py:560
  110.7 12.0 %collective-permute-start.9 = (bf16[216,256]{1,0:T(8,128)(2,1)S(1)}, bf16[216,256]{1,0:T(8,128)(2,1)S(1)}, u32[]{:S(2)}, u32[]{:S(2)}) collective-permute-start(bf16[216,256]{1,0:T(8,128)(2,1)S(1)} %add_convert_fusion.own_ref), channel_id=1, source_target_pairs={{0,1},{1,2},{2,3},{3,0},{4,5},{5,6},{6,7},{7,4},{8,9},{9,10},{10,1... | collective-permute-start | bytes 331784 | tf_op jit(solution)/shard_map/ppermute | solution.py:560
  115.0 5.3 %collective-permute-start.4 = (bf16[216,256]{1,0:T(8,128)(2,1)S(1)}, bf16[216,256]{1,0:T(8,128)(2,1)S(1)}, u32[]{:S(2)}, u32[]{:S(2)}) collective-permute-start(bf16[216,256]{1,0:T(8,128)(2,1)S(1)} %add_convert_fusion.1.own_ref), channel_id=1, source_target_pairs={{0,3},{1,0},{2,1},{3,2},{4,7},{5,4},{6,5},{7,6},{8,11},{9,8},{10,9... | collective-permute-start | bytes 331784 | tf_op jit(solution)/shard_map/ppermute | solution.py:560
  116.8 6.0 %collective-permute-start.11 = (bf16[216,256]{1,0:T(8,128)(2,1)S(1)}, bf16[216,256]{1,0:T(8,128)(2,1)S(1)}, u32[]{:S(2)}, u32[]{:S(2)}) collective-permute-start(bf16[216,256]{1,0:T(8,128)(2,1)S(1)} %collective-permute-done.10.third_ref), channel_id=1, source_target_pairs={{0,3},{1,0},{2,1},{3,2},{4,7},{5,4},{6,5},{7,6},{8,11},{9,8},{10,9... | collective-permute-start | bytes 331784 | tf_op jit(solution)/shard_map/ppermute | solution.py:560
  117.6 8.0 %collective-permute-start.3 = (bf16[216,256]{1,0:T(8,128)(2,1)S(1)}, bf16[216,256]{1,0:T(8,128)(2,1)S(1)}, u32[]{:S(2)}, u32[]{:S(2)}) collective-permute-start(bf16[216,256]{1,0:T(8,128)(2,1)S(1)} %add_convert_fusion.1.own_ref), channel_id=1, source_target_pairs={{0,1},{1,2},{2,3},{3,0},{4,5},{5,6},{6,7},{7,4},{8,9},{9,10},{10,1... | collective-permute-start | bytes 331784 | tf_op jit(solution)/shard_map/ppermute | solution.py:560
  120.2 5.4 %collective-permute-start.5 = (bf16[216,256]{1,0:T(8,128)(2,1)S(1)}, bf16[216,256]{1,0:T(8,128)(2,1)S(1)}, u32[]{:S(2)}, u32[]{:S(2)}) collective-permute-start(bf16[216,256]{1,0:T(8,128)(2,1)S(1)} %collective-permute-done.4.third_ref), channel_id=1, source_target_pairs={{0,3},{1,0},{2,1},{3,2},{4,7},{5,4},{6,5},{7,6},{8,11},{9,8},{10,9... | collective-permute-start | bytes 331784 | tf_op jit(solution)/shard_map/ppermute | solution.py:560
where the time goes:
time: 130 us; the launch traced here: 129 us
  blocking collectives  50.8 us (39%)
  Pallas kernels  38.4 us (30%)
  starting transfers between devices  24 us (18%)
  waiting for transfers between devices  14.4 us (11%)
    all_to_all x1, blocking collectives, shards(): lax.all_to_all(outgoing, 'expert', split_axis=0, concat_axis=0, tiled=True)  35.2 us
    ppermute x12, starting transfers between devices, send(): lax.ppermute(value, 'dp', [(i, (i + distance) % copies) for i in range(co...  18.4 us
    all_to_all x1, blocking collectives, shards(): lax.all_to_all(raw_out, 'expert', split_axis=0, concat_axis=0, tiled=True)  15.6 us
    pallas_call x2, Pallas kernels, gradient(): pl.pallas_call(functools.partial(backward_kernel, h), grid_spec=pltpu.Pre...  14.4 us
    all_to_all x1, waiting for transfers between devices, shards(): lax.all_to_all(cot_out, 'expert', split_axis=0, concat_axis=0, tiled=True)  9.98 us
    pallas_call x1, Pallas kernels, shards(): pl.pallas_call(dispatch_kernel, out_shape=shape_of((places, THIRDS * 128)...  7.21 us
    pallas_call x2, Pallas kernels, update(): pl.pallas_call(adam_kernel, grid_spec=pltpu.PrefetchScalarGridSpec(num_sc...  5.79 us
    all_to_all x1, starting transfers between devices, shards(): lax.all_to_all(cot_out, 'expert', split_axis=0, concat_axis=0, tiled=True)  5.62 us
  transfers between devices with their start and end apart: 13, of which 4 were waited for; matrix products, arithmetic and copies ran while one was open for 0% of the time, Pallas kernels for 8%

commit v1 on v0

--- a/solution.py
+++ b/solution.py
@@ -348,7 +348,7 @@
     h,
     order_ref,
     x_ref,
-    acts_ref,
+    acts_in,
     cot_in_ref,
     weights_ref,
     own_ref,
@@ -357,13 +357,22 @@
     third_ref,
     total_ref,
     cot_ref,
+    acts_ref,
+    sems,
 ):
     third = pl.program_id(0)
     groups = cot_ref.shape[0]
     rows = x_ref.shape[0]
 
+    def move(j, k):
+        source = acts_in.at[k, pl.ds(j * rows, rows), :]
+        return pltpu.make_async_copy(source, acts_ref.at[j, k], sems.at[j, k])
+
     @pl.when(third == 0)
     def _():
+        for j in range(THIRDS):
+            for k in reversed(range(LAYERS)):
+                move(j, k).start()
         cot_ref[...] = cot_in_ref[...].astype(F32)
         total_ref[...] = jnp.zeros_like(total_ref)
         lines = []
@@ -387,7 +396,8 @@
     lane = iota((1, 128), 1)
     wide_lane = iota((1, NET_WIDTH), 1)
     head = weights_ref[0, HEAD_ROW:PARAM_ROWS, :].astype(F32)
-    outer = mul(spread, acts_ref[LAYERS - 1], TN)[h * 64 : (h + 1) * 64]
+    move(third, LAYERS - 1).wait()
+    outer = mul(spread, acts_ref[third, LAYERS - 1], TN)[h * 64 : (h + 1) * 64]
     head_grad = jnp.sum(outer.reshape(4, DEPTH, NET_WIDTH), axis=1)
     bias_head = jnp.zeros((1, NET_WIDTH), F32)
     for c in range(4):
@@ -396,12 +406,15 @@
     up = mul(spread, head_tile(head, h))
     bias_lines = [None] * LAYERS
     for k in reversed(range(LAYERS)):
-        pre_grad = jnp.where(acts_ref[k].astype(F32) > 0, up, 0.0).astype(BF16)
+        pre_grad = jnp.where(acts_ref[third, k].astype(F32) > 0, up, 0.0).astype(BF16)
         bias_lines[k] = jnp.sum(pre_grad.astype(F32), axis=0, keepdims=True)
         if k > 0:
             start = ENC_WIDTH + (k - 1) * NET_WIDTH
-            total_ref[start : start + NET_WIDTH, :] += mul(acts_ref[k - 1], pre_grad, TN)
             up = mul(pre_grad, weights_ref[0, start : start + NET_WIDTH, :], NT)
+            move(third, k - 1).wait()
+            total_ref[start : start + NET_WIDTH, :] += mul(
+                acts_ref[third, k - 1], pre_grad, TN
+            )
         else:
             total_ref[0:ENC_WIDTH, :] += mul(x_ref[...], pre_grad, TN)[
                 h * ENC_WIDTH : (h + 1) * ENC_WIDTH
@@ -421,29 +434,30 @@
             share_ref[...] = total_ref[pl.ds(start, quarter), :].astype(share_ref.dtype)
 
 
-def adam_kernel(
-    order_ref,
-    own_ref,
-    first_ref,
-    second_ref,
-    third_ref,
-    param_ref,
-    one_ref,
-    two_ref,
-    *refs,
-):
-    step = pl.program_id(0)
-    new_param_ref, new_one_ref, new_two_ref = refs[-3:]
+def adam_kernel(h, order_ref, own_ref, first_ref, second_ref, third_ref, *refs):
+    olds, outs = refs[:3], refs[-8:-5]
+    grad_ref, *new_refs = refs[-5:-1]
+    sems = refs[-1]
+    quarter = own_ref.shape[0]
     for k, share_ref in enumerate((own_ref, first_ref, second_ref, third_ref)):
-
-        @pl.when(step == k)
-        def _():
-            new_param, new_one, new_two = adam_update(
-                param_ref[0], share_ref[...].astype(F32), one_ref[0], two_ref[0]
+        start = pl.multiple_of(order_ref[k] * quarter, 8)
+        grad_ref[pl.ds(start, quarter), :] = share_ref[...].astype(F32)
+    moves = []
+    size = PARAM_ROWS // 2
+    for part in range(2):
+        span = slice(part * size, (part + 1) * size)
+        values = adam_update(
+            olds[0][h, span, :], grad_ref[span, :], olds[1][h, span, :], olds[2][h, span, :]
+        )
+        for i in range(3):
+            new_refs[i][span, :] = values[i]
+            move = pltpu.make_async_copy(
+                new_refs[i].at[span], outs[i].at[h, span], sems.at[i, part]
             )
-            new_param_ref[0] = new_param
-            new_one_ref[0] = new_one
-            new_two_ref[0] = new_two
+            move.start()
+            moves.append(move)
+    for move in moves:
+        move.wait()
 
 
 def cost(micros):
@@ -567,7 +581,7 @@
                 grid=(THIRDS,),
                 in_specs=[
                     pl.BlockSpec((places, 128), lambda i, order: (0, i)),
-                    pl.BlockSpec((LAYERS, places, NET_WIDTH), lambda i, order: (0, i, 0)),
+                    anywhere,
                     lent(groups, 8, 128),
                     pl.BlockSpec((1, PARAM_ROWS, NET_WIDTH), lambda i, order: (h, 0, 0)),
                 ],
@@ -575,6 +589,8 @@
                 scratch_shapes=[
                     pltpu.VMEM((copies * quarter, NET_WIDTH), F32),
                     pltpu.VMEM((groups, 8, 128), F32),
+                    pltpu.VMEM((THIRDS, LAYERS, places, NET_WIDTH), BF16),
+                    pltpu.SemaphoreType.DMA((THIRDS, LAYERS)),
                 ],
             ),
             out_shape=[shape_of((quarter, NET_WIDTH), F32)]
@@ -593,18 +609,16 @@
         return share, behind, send(ahead, 3), ahead
 
     def update(h, pieces, earlier):
-        block = pl.BlockSpec((1, quarter, NET_WIDTH), lambda i, order: (h, order[i], 0))
         return pl.pallas_call(
-            adam_kernel,
-            grid_spec=pltpu.PrefetchScalarGridSpec(
-                num_scalar_prefetch=1,
-                grid=(copies,),
-                in_specs=[lent(quarter, NET_WIDTH)] * 4
-                + [block] * 3
-                + [pl.BlockSpec(memory_space=pl.ANY)] * len(earlier),
-                out_specs=[block] * 3,
-            ),
+            functools.partial(adam_kernel, h),
+            in_specs=[pl.BlockSpec(memory_space=pltpu.SMEM)]
+            + [vmem] * 7
+            + [anywhere] * len(earlier),
+            out_specs=[anywhere] * 3,
             out_shape=[shape_of(params.shape, F32)] * 3,
+            scratch_shapes=[pltpu.VMEM((copies * quarter, NET_WIDTH), F32)]
+            + [pltpu.VMEM((PARAM_ROWS, NET_WIDTH), F32)] * 3
+            + [pltpu.SemaphoreType.DMA((3, 2))],
             input_output_aliases={8 + i: i for i in range(len(earlier))},
             compiler_params=limits(12),
             cost_estimate=cost(2.0),

time: 130 us -> 133 us (1.023)
  Pallas kernels: 38.4 us -> 41.5 us
    pallas_call x2, Pallas kernels: 14.4 us -> 17.6 us  [gradient(): pl.pallas_call(functools.partial(backward_kernel, h), grid_spec=pltpu.Pre...]
  transfers between devices with their start and end apart: 13 -> 13, of which waited for: 4 -> 4; matrix products, arithmetic and copies ran while one was open for 0% -> 0% of each run, Pallas kernels for 8% -> 9%
where the time goes in v1:
time: 133 us; the launch traced here: 132 us
  blocking collectives  50.8 us (38%)
  Pallas kernels  41.5 us (31%)
  starting transfers between devices  23.9 us (18%)
  waiting for transfers between devices  14.3 us (11%)
    all_to_all x1, blocking collectives, shards(): lax.all_to_all(outgoing, 'expert', split_axis=0, concat_axis=0, tiled=True)  35.2 us
    ppermute x12, starting transfers between devices, send(): lax.ppermute(value, 'dp', [(i, (i + distance) % copies) for i in range(co...  18.3 us
    pallas_call x2, Pallas kernels, gradient(): pl.pallas_call(functools.partial(backward_kernel, h), grid_spec=pltpu.Pre...  17.6 us
    all_to_all x1, blocking collectives, shards(): lax.all_to_all(raw_out, 'expert', split_axis=0, concat_axis=0, tiled=True)  15.6 us
    all_to_all x1, waiting for transfers between devices, shards(): lax.all_to_all(cot_out, 'expert', split_axis=0, concat_axis=0, tiled=True)  9.98 us
    pallas_call x1, Pallas kernels, shards(): pl.pallas_call(dispatch_kernel, out_shape=shape_of((places, THIRDS * 128)...  7.21 us
    pallas_call x2, Pallas kernels, update(): pl.pallas_call(functools.partial(adam_kernel, h), in_specs=[pl.BlockSpec(...  5.71 us
    all_to_all x1, starting transfers between devices, shards(): lax.all_to_all(cot_out, 'expert', split_axis=0, concat_axis=0, tiled=True)  5.62 us
  transfers between devices with their start and end apart: 13, of which 4 were waited for; matrix products, arithmetic and copies ran while one was open for 0% of the time, Pallas kernels for 9%

profile of v1, /device:TPU:2, one launch (start us, length us, event | category | flops | bytes accessed | tf_op | source)
XLA Modules:
  0.0 131.7 jit_solution(3121565807928593484)
XLA Ops:
  0.6 0.0 copy-start
  0.6 7.2 %dispatch.1 = bf16[1024,384]{1,0:T(8,128)(2,1)} custom-call(bf16[32,64,128]{2,1,0:T(8,128)(2,1)} %bitcast.20, s32[32,128]{1,0:T(8,128)} %bitcast.12, s32[32,128]{1,0:T(8,128)} %bitcast.14), custom_call_target="tpu_custom_call" | custom-call | tf_op jit(solution)/shard_map/dispatch/pallas_call | solution.py:496
  7.9 35.2 %all_to_all.21 = bf16[64,16,384]{2,1,0:T(8,128)(2,1)S(1)} all-to-all(bf16[64,16,384]{2,1,0:T(8,128)(2,1)} %bitcast.19), channel_id=1, replica_groups=mesh['expert'=64,'dp'=4] {'expert'}, dimensions={0} | all-to-all | bytes 1572864 | tf_op jit(solution)/shard_map/all_to_all | solution.py:511
  43.1 0.0 copy-start.7
  43.1 0.0 copy-start.8
  43.1 0.0 copy-start.9
  43.1 0.0 copy-start.10
  43.1 0.0 copy-start.11
  43.1 0.0 copy-done
  43.1 5.5 %forward.1 = (bf16[4,3072,256]{2,1,0:T(8,128)(2,1)}, bf16[4,3072,256]{2,1,0:T(8,128)(2,1)}, bf16[64,8,128]{2,1,0:T(8,128)(2,1)S(1)}, bf16[2,848,256]{2,1,0:T(8,128)(2,1)S(1)}) custom-call(bf16[1024,384]{1,0:T(8,128)(2,1)S(1)} %bitcast.9, f32[2,848,256]{2,1,0:T(8,128)S(1)} %copy-done), custom_call_target="tpu_custom_call" | custom-call | tf_op jit(solution)/shard_map/forward/pallas_call | solution.py:517
  48.7 15.6 %all_to_all.22.back_ref = bf16[64,8,128]{2,1,0:T(8,128)(2,1)S(1)} all-to-all(bf16[64,8,128]{2,1,0:T(8,128)(2,1)S(1)} %get-tuple-element.30), channel_id=1, replica_groups=mesh['expert'=64,'dp'=4] {'expert'}, dimensions={0} | all-to-all | bytes 262144 | tf_op jit(solution)/shard_map/all_to_all | solution.py:534
  64.3 0.0 copy-done.3
  64.3 0.0 copy-done.4
  64.3 0.0 copy-done.5
  64.3 0.0 copy-done.6
  64.3 5.4 %rays.1 = (bf16[64,8,128]{2,1,0:T(8,128)(2,1)}, f32[1,128]{1,0:T(1,128)}, f32[16,64]{1,0:T(8,128)}, f32[16,64]{1,0:T(8,128)}, f32[16,64]{1,0:T(8,128)}) custom-call(bf16[64,8,128]{2,1,0:T(8,128)(2,1)S(1)} %all_to_all.22.back_ref, s32[32,128]{1,0:T(8,128)S(1)} %bitcast.13, s32[32,128]{1,0:T(8,128)S(1)} %bitcast.15, s32[1,128]{1,0:T(1,128)S(1)} %bitcast.17, ...), custom_call_target="tpu_custom_call" | custom-call | tf_op jit(solution)/shard_map/rays/pallas_call | solution.py:537
  69.7 5.6 %all-to-all-start.2 = ((bf16[64,8,128]{2,1,0:T(8,128)(2,1)}), bf16[64,8,128]{2,1,0:T(8,128)(2,1)S(1)}, u32[]{:S(2)}, u32[]{:S(2)}) async-start(bf16[64,8,128]{2,1,0:T(8,128)(2,1)} %get-tuple-element.33), calls=%async_computation.2 | async-start | bytes 262144 | tf_op jit(solution)/shard_map/all_to_all | solution.py:565
  75.4 10.0 %all-to-all-done.2.cot_in_ref = bf16[64,8,128]{2,1,0:T(8,128)(2,1)S(1)} async-done(((bf16[64,8,128]{2,1,0:T(8,128)(2,1)}), bf16[64,8,128]{2,1,0:T(8,128)(2,1)S(1)}, u32[]{:S(2)}, u32[]{:S(2)}) %all-to-all-start.2) | async-done | bytes 131104 | tf_op jit(solution)/shard_map/all_to_all | solution.py:565
  85.4 8.6 %backward.3 = (f32[216,256]{1,0:T(8,128)S(1)}, bf16[216,256]{1,0:T(8,128)(2,1)S(1)}, bf16[216,256]{1,0:T(8,128)(2,1)S(1)}, bf16[216,256]{1,0:T(8,128)(2,1)S(1)}) custom-call(s32[4]{0:T(128)S(1)} %and_select_fusion.order_ref, bf16[1024,384]{1,0:T(8,128)(2,1)S(1)} %bitcast.10, bf16[4,3072,256]{2,1,0:T(8,128)(2,1)} %get-tuple-element.39.acts_in, ...), custom_call_target="tpu_custom_call" | custom-call | flops 6000000000 | bytes 18000000 | tf_op jit(solution)/shard_map/backward/pallas_call | solution.py:577
  94.0 3.3 %collective-permute-start.6 = (bf16[216,256]{1,0:T(8,128)(2,1)S(1)}, bf16[216,256]{1,0:T(8,128)(2,1)S(1)}, u32[]{:S(2)}, u32[]{:S(2)}) collective-permute-start(bf16[216,256]{1,0:T(8,128)(2,1)S(1)} %get-tuple-element.41), channel_id=1, source_target_pairs={{0,2},{1,3},{2,0},{3,1},{4,6},{5,7},{6,4},{7,5},{8,10},{9,11},{10,... | collective-permute-start | bytes 331784 | tf_op jit(solution)/shard_map/ppermute | solution.py:574
  97.3 0.7 collective-permute-start.7
  98.0 2.6 %collective-permute-start.8 = (bf16[216,256]{1,0:T(8,128)(2,1)S(1)}, bf16[216,256]{1,0:T(8,128)(2,1)S(1)}, u32[]{:S(2)}, u32[]{:S(2)}) collective-permute-start(bf16[216,256]{1,0:T(8,128)(2,1)S(1)} %get-tuple-element.43), channel_id=1, source_target_pairs={{0,3},{1,0},{2,1},{3,2},{4,7},{5,4},{6,5},{7,6},{8,11},{9,8},{10,9... | collective-permute-start | bytes 331784 | tf_op jit(solution)/shard_map/ppermute | solution.py:574
  100.5 9.0 %backward.2 = (f32[216,256]{1,0:T(8,128)S(1)}, bf16[216,256]{1,0:T(8,128)(2,1)S(1)}, bf16[216,256]{1,0:T(8,128)(2,1)S(1)}, bf16[216,256]{1,0:T(8,128)(2,1)S(1)}) custom-call(s32[4]{0:T(128)S(1)} %and_select_fusion.order_ref, bf16[1024,384]{1,0:T(8,128)(2,1)S(1)} %bitcast.11, bf16[4,3072,256]{2,1,0:T(8,128)(2,1)} %get-tuple-element.32.acts_in, ...), custom_call_target="tpu_custom_call" | custom-call | flops 6000000000 | bytes 18000000 | tf_op jit(solution)/shard_map/backward/pallas_call | solution.py:577
  109.5 0.1 collective-permute-start
  109.6 0.8 collective-permute-start.1
  110.4 0.0 collective-permute-done.6
  110.5 2.5 %collective-permute-start.2 = (bf16[216,256]{1,0:T(8,128)(2,1)S(1)}, bf16[216,256]{1,0:T(8,128)(2,1)S(1)}, u32[]{:S(2)}, u32[]{:S(2)}) collective-permute-start(bf16[216,256]{1,0:T(8,128)(2,1)S(1)} %get-tuple-element.38), channel_id=1, source_target_pairs={{0,3},{1,0},{2,1},{3,2},{4,7},{5,4},{6,5},{7,6},{8,11},{9,8},{10,9... | collective-permute-start | bytes 331784 | tf_op jit(solution)/shard_map/ppermute | solution.py:574
  112.9 0.0 collective-permute-done.7
  112.9 0.0 collective-permute-done.8
  112.9 0.1 add_convert_fusion.own_ref
  113.0 1.1 collective-permute-start.10
  114.1 1.2 collective-permute-start.9
  115.3 1.5 %collective-permute-done = bf16[216,256]{1,0:T(8,128)(2,1)S(1)} collective-permute-done((bf16[216,256]{1,0:T(8,128)(2,1)S(1)}, bf16[216,256]{1,0:T(8,128)(2,1)S(1)}, u32[]{:S(2)}, u32[]{:S(2)}) %collective-permute-start) | collective-permute-done | bytes 110624 | tf_op jit(solution)/shard_map/ppermute | solution.py:574
  116.8 1.3 collective-permute-done.1
  118.1 0.0 collective-permute-done.2
  118.1 0.1 add_convert_fusion.1.own_ref
  118.1 1.6 %collective-permute-start.4 = (bf16[216,256]{1,0:T(8,128)(2,1)S(1)}, bf16[216,256]{1,0:T(8,128)(2,1)S(1)}, u32[]{:S(2)}, u32[]{:S(2)}) collective-permute-start(bf16[216,256]{1,0:T(8,128)(2,1)S(1)} %add_convert_fusion.1.own_ref), channel_id=1, source_target_pairs={{0,3},{1,0},{2,1},{3,2},{4,7},{5,4},{6,5},{7,6},{8,11},{9,8},{10,9... | collective-permute-start | bytes 331784 | tf_op jit(solution)/shard_map/ppermute | solution.py:574
  119.8 0.0 collective-permute-done.10.third_ref
  119.8 1.0 collective-permute-start.11
  120.8 1.0 collective-permute-start.3
  121.8 1.5 %collective-permute-done.4.third_ref = bf16[216,256]{1,0:T(8,128)(2,1)S(1)} collective-permute-done((bf16[216,256]{1,0:T(8,128)(2,1)S(1)}, bf16[216,256]{1,0:T(8,128)(2,1)S(1)}, u32[]{:S(2)}, u32[]{:S(2)}) %collective-permute-start.4) | collective-permute-done | bytes 110624 | tf_op jit(solution)/shard_map/ppermute | solution.py:574
  123.3 2.4 %collective-permute-start.5 = (bf16[216,256]{1,0:T(8,128)(2,1)S(1)}, bf16[216,256]{1,0:T(8,128)(2,1)S(1)}, u32[]{:S(2)}, u32[]{:S(2)}) collective-permute-start(bf16[216,256]{1,0:T(8,128)(2,1)S(1)} %collective-permute-done.4.third_ref), channel_id=1, source_target_pairs={{0,3},{1,0},{2,1},{3,2},{4,7},{5,4},{6,5},{7,6},{8,11},{9,8},{10,9... | collective-permute-start | bytes 331784 | tf_op jit(solution)/shard_map/ppermute | solution.py:574
  125.7 0.0 collective-permute-done.9.first_ref
  125.7 0.0 collective-permute-done.11.second_ref
  125.7 2.9 %adam.2 = (f32[2,848,256]{2,1,0:T(8,128)}, f32[2,848,256]{2,1,0:T(8,128)}, f32[2,848,256]{2,1,0:T(8,128)}) custom-call(s32[4]{0:T(128)S(1)} %and_select_fusion.1.order_ref, bf16[216,256]{1,0:T(8,128)(2,1)S(1)} %add_convert_fusion.own_ref, bf16[216,256]{1,0:T(8,128)(2,1)S(1)} %collective-permute-done.9.first_ref, ...), custom_call_target="tpu_custom_call" | custom-call | flops 2000000000 | bytes 6000000 | tf_op jit(solution)/shard_map/adam/pallas_call | solution.py:612
  128.6 0.0 collective-permute-done.3.first_ref
  128.6 0.0 collective-permute-done.5.second_ref
  128.6 2.9 %adam.3 = (f32[2,848,256]{2,1,0:T(8,128)}, f32[2,848,256]{2,1,0:T(8,128)}, f32[2,848,256]{2,1,0:T(8,128)}) custom-call(s32[4]{0:T(128)S(1)} %and_select_fusion.1.order_ref, bf16[216,256]{1,0:T(8,128)(2,1)S(1)} %add_convert_fusion.1.own_ref, ...), custom_call_target="tpu_custom_call", output_to_operand_aliasing={{0}: (8, {}), {1}: (9, {}), {2}: (10, {})} | custom-call | flops 2000000000 | bytes 6000000 | tf_op jit(solution)/shard_map/adam/pallas_call | solution.py:612
  (15 shorter events, 0.0 us)
Async XLA Ops:
  0.6 42.5 %copy-start = (f32[2,848,256]{2,1,0:T(8,128)S(1)}, f32[2,848,256]{2,1,0:T(8,128)}, u32[]{:S(2)}) copy-start(f32[2,848,256]{2,1,0:T(8,128)} %refs_0_.3) | copy-start | bytes 5210116
  43.1 21.2 %copy-start.3 = (s32[128,32]{0,1:T(8,128)S(1)}, s32[128,32]{0,1:T(8,128)}, u32[]{:S(2)}) copy-start(s32[128,32]{0,1:T(8,128)} %param.17) | copy-start | bytes 49156
  43.1 21.2 %copy-start.4 = (s32[128,32]{0,1:T(8,128)S(1)}, s32[128,32]{0,1:T(8,128)}, u32[]{:S(2)}) copy-start(s32[128,32]{0,1:T(8,128)} %param.18) | copy-start | bytes 49156
  43.1 21.2 %copy-start.5 = (f32[128,32]{0,1:T(8,128)S(1)}, f32[128,32]{0,1:T(8,128)}, u32[]{:S(2)}) copy-start(f32[128,32]{0,1:T(8,128)} %param.14) | copy-start | bytes 49156
  43.1 21.2 %copy-start.6 = (f32[16,64]{1,0:T(8,128)S(1)}, f32[16,64]{1,0:T(8,128)}, u32[]{:S(2)}) copy-start(f32[16,64]{1,0:T(8,128)} %code_ref.1) | copy-start | bytes 12292
  43.1 21.2 %copy-start.7 = (f32[16,64]{1,0:T(8,128)S(1)}, f32[16,64]{1,0:T(8,128)}, u32[]{:S(2)}) copy-start(f32[16,64]{1,0:T(8,128)} %first_ref.1) | copy-start | bytes 12292
  43.1 21.2 %copy-start.8 = (f32[16,64]{1,0:T(8,128)S(1)}, f32[16,64]{1,0:T(8,128)}, u32[]{:S(2)}) copy-start(f32[16,64]{1,0:T(8,128)} %second_ref.1) | copy-start | bytes 12292
  43.1 21.2 %copy-start.9 = (f32[3,128]{1,0:T(4,128)S(1)}, f32[3,128]{1,0:T(4,128)}, u32[]{:S(2)}) copy-start(f32[3,128]{1,0:T(4,128)} %targets_ref.1) | copy-start | bytes 4612
  43.1 21.2 %copy-start.10 = (s32[128]{0:T(128)S(1)}, s32[128]{0:T(128)}, u32[]{:S(2)}) copy-start(s32[128]{0:T(128)} %param.19) | copy-start | bytes 1540
  43.1 21.2 %copy-start.11 = (s32[128]{0:T(128)S(1)}, s32[128]{0:T(128)}, u32[]{:S(2)}) copy-start(s32[128]{0:T(128)} %param.16) | copy-start | bytes 1540
  69.7 15.6 %all-to-all-start.2 = ((bf16[64,8,128]{2,1,0:T(8,128)(2,1)}), bf16[64,8,128]{2,1,0:T(8,128)(2,1)S(1)}, u32[]{:S(2)}, u32[]{:S(2)}) async-start(bf16[64,8,128]{2,1,0:T(8,128)(2,1)} %get-tuple-element.33), calls=%async_computation.2 | async-start | bytes 262144 | tf_op jit(solution)/shard_map/all_to_all | solution.py:565
  94.0 16.4 %collective-permute-start.6 = (bf16[216,256]{1,0:T(8,128)(2,1)S(1)}, bf16[216,256]{1,0:T(8,128)(2,1)S(1)}, u32[]{:S(2)}, u32[]{:S(2)}) collective-permute-start(bf16[216,256]{1,0:T(8,128)(2,1)S(1)} %get-tuple-element.41), channel_id=1, source_target_pairs={{0,2},{1,3},{2,0},{3,1},{4,6},{5,7},{6,4},{7,5},{8,10},{9,11},{10,... | collective-permute-start | bytes 331784 | tf_op jit(solution)/shard_map/ppermute | solution.py:574
  97.3 15.6 %collective-permute-start.7 = (bf16[216,256]{1,0:T(8,128)(2,1)S(1)}, bf16[216,256]{1,0:T(8,128)(2,1)S(1)}, u32[]{:S(2)}, u32[]{:S(2)}) collective-permute-start(bf16[216,256]{1,0:T(8,128)(2,1)S(1)} %get-tuple-element.42), channel_id=1, source_target_pairs={{0,1},{1,2},{2,3},{3,0},{4,5},{5,6},{6,7},{7,4},{8,9},{9,10},{10,1... | collective-permute-start | bytes 331784 | tf_op jit(solution)/shard_map/ppermute | solution.py:574
  98.0 15.0 %collective-permute-start.8 = (bf16[216,256]{1,0:T(8,128)(2,1)S(1)}, bf16[216,256]{1,0:T(8,128)(2,1)S(1)}, u32[]{:S(2)}, u32[]{:S(2)}) collective-permute-start(bf16[216,256]{1,0:T(8,128)(2,1)S(1)} %get-tuple-element.43), channel_id=1, source_target_pairs={{0,3},{1,0},{2,1},{3,2},{4,7},{5,4},{6,5},{7,6},{8,11},{9,8},{10,9... | collective-permute-start | bytes 331784 | tf_op jit(solution)/shard_map/ppermute | solution.py:574
  100.5 25.2 %copy-start.1 = (f32[2,848,256]{2,1,0:T(8,128)S(1)}, f32[2,848,256]{2,1,0:T(8,128)}, u32[]{:S(2)}) copy-start(f32[2,848,256]{2,1,0:T(8,128)} %refs_1_.3) | copy-start | bytes 5210116
  100.5 25.2 %copy-start.2 = (f32[2,848,256]{2,1,0:T(8,128)S(1)}, f32[2,848,256]{2,1,0:T(8,128)}, u32[]{:S(2)}) copy-start(f32[2,848,256]{2,1,0:T(8,128)} %refs_2_.3) | copy-start | bytes 5210116
  109.5 7.3 %collective-permute-start = (bf16[216,256]{1,0:T(8,128)(2,1)S(1)}, bf16[216,256]{1,0:T(8,128)(2,1)S(1)}, u32[]{:S(2)}, u32[]{:S(2)}) collective-permute-start(bf16[216,256]{1,0:T(8,128)(2,1)S(1)} %get-tuple-element.36), channel_id=1, source_target_pairs={{0,2},{1,3},{2,0},{3,1},{4,6},{5,7},{6,4},{7,5},{8,10},{9,11},{10,... | collective-permute-start | bytes 331784 | tf_op jit(solution)/shard_map/ppermute | solution.py:574
  109.6 8.5 %collective-permute-start.1 = (bf16[216,256]{1,0:T(8,128)(2,1)S(1)}, bf16[216,256]{1,0:T(8,128)(2,1)S(1)}, u32[]{:S(2)}, u32[]{:S(2)}) collective-permute-start(bf16[216,256]{1,0:T(8,128)(2,1)S(1)} %get-tuple-element.37), channel_id=1, source_target_pairs={{0,1},{1,2},{2,3},{3,0},{4,5},{5,6},{6,7},{7,4},{8,9},{9,10},{10,1... | collective-permute-start | bytes 331784 | tf_op jit(solution)/shard_map/ppermute | solution.py:574
  110.5 7.6 %collective-permute-start.2 = (bf16[216,256]{1,0:T(8,128)(2,1)S(1)}, bf16[216,256]{1,0:T(8,128)(2,1)S(1)}, u32[]{:S(2)}, u32[]{:S(2)}) collective-permute-start(bf16[216,256]{1,0:T(8,128)(2,1)S(1)} %get-tuple-element.38), channel_id=1, source_target_pairs={{0,3},{1,0},{2,1},{3,2},{4,7},{5,4},{6,5},{7,6},{8,11},{9,8},{10,9... | collective-permute-start | bytes 331784 | tf_op jit(solution)/shard_map/ppermute | solution.py:574
  113.0 6.8 %collective-permute-start.10 = (bf16[216,256]{1,0:T(8,128)(2,1)S(1)}, bf16[216,256]{1,0:T(8,128)(2,1)S(1)}, u32[]{:S(2)}, u32[]{:S(2)}) collective-permute-start(bf16[216,256]{1,0:T(8,128)(2,1)S(1)} %add_convert_fusion.own_ref), channel_id=1, source_target_pairs={{0,3},{1,0},{2,1},{3,2},{4,7},{5,4},{6,5},{7,6},{8,11},{9,8},{10,9... | collective-permute-start | bytes 331784 | tf_op jit(solution)/shard_map/ppermute | solution.py:574
  114.1 11.6 %collective-permute-start.9 = (bf16[216,256]{1,0:T(8,128)(2,1)S(1)}, bf16[216,256]{1,0:T(8,128)(2,1)S(1)}, u32[]{:S(2)}, u32[]{:S(2)}) collective-permute-start(bf16[216,256]{1,0:T(8,128)(2,1)S(1)} %add_convert_fusion.own_ref), channel_id=1, source_target_pairs={{0,1},{1,2},{2,3},{3,0},{4,5},{5,6},{6,7},{7,4},{8,9},{9,10},{10,1... | collective-permute-start | bytes 331784 | tf_op jit(solution)/shard_map/ppermute | solution.py:574
  118.1 5.2 %collective-permute-start.4 = (bf16[216,256]{1,0:T(8,128)(2,1)S(1)}, bf16[216,256]{1,0:T(8,128)(2,1)S(1)}, u32[]{:S(2)}, u32[]{:S(2)}) collective-permute-start(bf16[216,256]{1,0:T(8,128)(2,1)S(1)} %add_convert_fusion.1.own_ref), channel_id=1, source_target_pairs={{0,3},{1,0},{2,1},{3,2},{4,7},{5,4},{6,5},{7,6},{8,11},{9,8},{10,9... | collective-permute-start | bytes 331784 | tf_op jit(solution)/shard_map/ppermute | solution.py:574
  119.8 6.0 %collective-permute-start.11 = (bf16[216,256]{1,0:T(8,128)(2,1)S(1)}, bf16[216,256]{1,0:T(8,128)(2,1)S(1)}, u32[]{:S(2)}, u32[]{:S(2)}) collective-permute-start(bf16[216,256]{1,0:T(8,128)(2,1)S(1)} %collective-permute-done.10.third_ref), channel_id=1, source_target_pairs={{0,3},{1,0},{2,1},{3,2},{4,7},{5,4},{6,5},{7,6},{8,11},{9,8},{10,9... | collective-permute-start | bytes 331784 | tf_op jit(solution)/shard_map/ppermute | solution.py:574
  120.8 7.8 %collective-permute-start.3 = (bf16[216,256]{1,0:T(8,128)(2,1)S(1)}, bf16[216,256]{1,0:T(8,128)(2,1)S(1)}, u32[]{:S(2)}, u32[]{:S(2)}) collective-permute-start(bf16[216,256]{1,0:T(8,128)(2,1)S(1)} %add_convert_fusion.1.own_ref), channel_id=1, source_target_pairs={{0,1},{1,2},{2,3},{3,0},{4,5},{5,6},{6,7},{7,4},{8,9},{9,10},{10,1... | collective-permute-start | bytes 331784 | tf_op jit(solution)/shard_map/ppermute | solution.py:574
  123.3 5.3 %collective-permute-start.5 = (bf16[216,256]{1,0:T(8,128)(2,1)S(1)}, bf16[216,256]{1,0:T(8,128)(2,1)S(1)}, u32[]{:S(2)}, u32[]{:S(2)}) collective-permute-start(bf16[216,256]{1,0:T(8,128)(2,1)S(1)} %collective-permute-done.4.third_ref), channel_id=1, source_target_pairs={{0,3},{1,0},{2,1},{3,2},{4,7},{5,4},{6,5},{7,6},{8,11},{9,8},{10,9... | collective-permute-start | bytes 331784 | tf_op jit(solution)/shard_map/ppermute | solution.py:574

commit v2 on v0

--- a/solution.py
+++ b/solution.py
@@ -421,25 +421,16 @@
             share_ref[...] = total_ref[pl.ds(start, quarter), :].astype(share_ref.dtype)
 
 
-def adam_kernel(
-    order_ref,
-    own_ref,
-    first_ref,
-    second_ref,
-    third_ref,
-    param_ref,
-    one_ref,
-    two_ref,
-    *refs,
-):
+def adam_kernel(count, order_ref, *refs):
     step = pl.program_id(0)
+    param_ref, one_ref, two_ref = refs[count : count + 3]
     new_param_ref, new_one_ref, new_two_ref = refs[-3:]
-    for k, share_ref in enumerate((own_ref, first_ref, second_ref, third_ref)):
+    for k in range(count):
 
         @pl.when(step == k)
         def _():
             new_param, new_one, new_two = adam_update(
-                param_ref[0], share_ref[...].astype(F32), one_ref[0], two_ref[0]
+                param_ref[0], refs[k][...].astype(F32), one_ref[0], two_ref[0]
             )
             new_param_ref[0] = new_param
             new_one_ref[0] = new_one
@@ -590,27 +581,30 @@
             share = share + send(shares[k], k).astype(F32)
         share = share.astype(BF16)
         behind, ahead = send(share, 1), send(share, 3)
-        return share, behind, send(ahead, 3), ahead
-
-    def update(h, pieces, earlier):
-        block = pl.BlockSpec((1, quarter, NET_WIDTH), lambda i, order: (h, order[i], 0))
+        return share, behind, ahead, send(ahead, 3)
+
+    def update(pieces, turns, micros, earlier):
+        count, each = len(pieces), len(turns)
+        block = pl.BlockSpec(
+            (1, quarter, NET_WIDTH), lambda i, order: (i // each, order[i % each], 0)
+        )
         return pl.pallas_call(
-            adam_kernel,
+            functools.partial(adam_kernel, count),
             grid_spec=pltpu.PrefetchScalarGridSpec(
                 num_scalar_prefetch=1,
-                grid=(copies,),
-                in_specs=[lent(quarter, NET_WIDTH)] * 4
+                grid=(count,),
+                in_specs=[lent(quarter, NET_WIDTH)] * count
                 + [block] * 3
-                + [pl.BlockSpec(memory_space=pl.ANY)] * len(earlier),
+                + [anywhere] * len(earlier),
                 out_specs=[block] * 3,
             ),
             out_shape=[shape_of(params.shape, F32)] * 3,
-            input_output_aliases={8 + i: i for i in range(len(earlier))},
-            compiler_params=limits(12),
-            cost_estimate=cost(2.0),
+            input_output_aliases={count + 4 + i: i for i in range(len(earlier))},
+            compiler_params=limits(58),
+            cost_estimate=cost(micros),
             name="adam",
         )(
-            (position - turns) % copies,
+            (position + jnp.array(turns, jnp.int32)) % copies,
             *pieces,
             params,
             first_moment,
@@ -619,8 +613,11 @@
         )
 
     pieces = [collect(gradient(h)) for h in range(2)]
-    updated = update(0, pieces[0], ())
-    new_params, new_first, new_second = update(1, pieces[1], updated)
+    near = pieces[0][:3] + pieces[1][:3]
+    updated = update(near, (0, copies - 1, 1), 4.0, ())
+    new_params, new_first, new_second = update(
+        (pieces[0][3], pieces[1][3]), (2,), 1.5, updated
+    )
     return (
         loss.reshape(RAYS),
         new_params,

time: 130 us -> 136 us (1.046); the launches traced: 129 us -> 136 us
  Pallas kernels: 38.4 us -> 42.1 us
  local copies, waits for them, and re-layouts: 0.06 us -> 1.96 us
    pallas_call x2, Pallas kernels: 5.79 us -> 9.81 us  [update(): pl.pallas_call(functools.partial(adam_kernel, count), grid_spec=pltpu.Pre...]
    unnamed x24 -> x38, local copies, waits for them, and re-layouts: 0.06 us -> 1.96 us
  transfers between devices with their start and end apart: 13 -> 13, of which waited for: 4 -> 4; matrix products, arithmetic and copies ran while one was open for 0% -> 0% of each run, Pallas kernels for 8% -> 10%
where the time goes in v2:
time: 136 us
  blocking collectives  50.8 us (37%)
  Pallas kernels  42.1 us (31%)
  starting transfers between devices  25.1 us (18%)
  waiting for transfers between devices  14.5 us (11%)
  local copies, waits for them, and re-layouts  1.96 us (1%)
    all_to_all x1, blocking collectives, shards(): lax.all_to_all(outgoing, 'expert', split_axis=0, concat_axis=0, tiled=True)  35.2 us
    ppermute x12, starting transfers between devices, send(): lax.ppermute(value, 'dp', [(i, (i + distance) % copies) for i in range(co...  19.4 us
    all_to_all x1, blocking collectives, shards(): lax.all_to_all(raw_out, 'expert', split_axis=0, concat_axis=0, tiled=True)  15.6 us
    pallas_call x2, Pallas kernels, gradient(): pl.pallas_call(functools.partial(backward_kernel, h), grid_spec=pltpu.Pre...  14.1 us
    all_to_all x1, waiting for transfers between devices, shards(): lax.all_to_all(cot_out, 'expert', split_axis=0, concat_axis=0, tiled=True)  9.98 us
    pallas_call x2, Pallas kernels, update(): pl.pallas_call(functools.partial(adam_kernel, count), grid_spec=pltpu.Pre...  9.81 us
    pallas_call x1, Pallas kernels, shards(): pl.pallas_call(dispatch_kernel, out_shape=shape_of((places, THIRDS * 128)...  7.21 us
    all_to_all x1, starting transfers between devices, shards(): lax.all_to_all(cot_out, 'expert', split_axis=0, concat_axis=0, tiled=True)  5.63 us
  transfers between devices with their start and end apart: 13, of which 4 were waited for; matrix products, arithmetic and copies ran while one was open for 0% of the time, Pallas kernels for 10%

profile of v2, /device:TPU:2, one launch (start us, length us, event | category | flops | bytes accessed | tf_op | source)
XLA Modules:
  0.0 136.0 jit_solution(13948157593412181215)
XLA Ops:
  0.6 0.0 copy-start
  0.6 7.2 %dispatch.1 = bf16[1024,384]{1,0:T(8,128)(2,1)} custom-call(bf16[32,64,128]{2,1,0:T(8,128)(2,1)} %bitcast.21, s32[32,128]{1,0:T(8,128)} %bitcast.13, s32[32,128]{1,0:T(8,128)} %bitcast.15), custom_call_target="tpu_custom_call" | custom-call | tf_op jit(solution)/shard_map/dispatch/pallas_call | solution.py:473
  7.9 35.2 %all_to_all.21 = bf16[64,16,384]{2,1,0:T(8,128)(2,1)S(1)} all-to-all(bf16[64,16,384]{2,1,0:T(8,128)(2,1)} %bitcast.20), channel_id=1, replica_groups=mesh['expert'=64,'dp'=4] {'expert'}, dimensions={0} | all-to-all | bytes 1572864 | tf_op jit(solution)/shard_map/all_to_all | solution.py:488
  43.1 0.0 copy-start.5
  43.1 0.0 copy-start.6
  43.1 0.0 copy-start.7
  43.1 0.0 copy-start.8
  43.1 0.0 copy-start.9
  43.1 5.6 %forward.1 = (bf16[4,3072,256]{2,1,0:T(8,128)(2,1)}, bf16[4,3072,256]{2,1,0:T(8,128)(2,1)}, bf16[64,8,128]{2,1,0:T(8,128)(2,1)S(1)}, bf16[2,848,256]{2,1,0:T(8,128)(2,1)S(1)}) custom-call(bf16[1024,384]{1,0:T(8,128)(2,1)S(1)} %bitcast.10, f32[2,848,256]{2,1,0:T(8,128)S(1)} %copy-done), custom_call_target="tpu_custom_call" | custom-call | tf_op jit(solution)/shard_map/forward/pallas_call | solution.py:494
  48.7 15.6 %all_to_all.22.back_ref = bf16[64,8,128]{2,1,0:T(8,128)(2,1)S(1)} all-to-all(bf16[64,8,128]{2,1,0:T(8,128)(2,1)S(1)} %get-tuple-element.30), channel_id=1, replica_groups=mesh['expert'=64,'dp'=4] {'expert'}, dimensions={0} | all-to-all | bytes 262144 | tf_op jit(solution)/shard_map/all_to_all | solution.py:511
  64.4 5.4 %rays.1 = (bf16[64,8,128]{2,1,0:T(8,128)(2,1)}, f32[1,128]{1,0:T(1,128)}, f32[16,64]{1,0:T(8,128)}, f32[16,64]{1,0:T(8,128)}, f32[16,64]{1,0:T(8,128)}) custom-call(bf16[64,8,128]{2,1,0:T(8,128)(2,1)S(1)} %all_to_all.22.back_ref, s32[32,128]{1,0:T(8,128)S(1)} %bitcast.14, s32[32,128]{1,0:T(8,128)S(1)} %bitcast.16, s32[1,128]{1,0:T(1,128)S(1)} %bitcast.18, ...), custom_call_target="tpu_custom_call" | custom-call | tf_op jit(solution)/shard_map/rays/pallas_call | solution.py:514
  69.7 5.6 %all-to-all-start.2 = ((bf16[64,8,128]{2,1,0:T(8,128)(2,1)}), bf16[64,8,128]{2,1,0:T(8,128)(2,1)S(1)}, u32[]{:S(2)}, u32[]{:S(2)}) async-start(bf16[64,8,128]{2,1,0:T(8,128)(2,1)} %get-tuple-element.33), calls=%async_computation.2 | async-start | bytes 262144 | tf_op jit(solution)/shard_map/all_to_all | solution.py:542
  75.4 10.0 %all-to-all-done.2.cot_in_ref = bf16[64,8,128]{2,1,0:T(8,128)(2,1)S(1)} async-done(((bf16[64,8,128]{2,1,0:T(8,128)(2,1)}), bf16[64,8,128]{2,1,0:T(8,128)(2,1)S(1)}, u32[]{:S(2)}, u32[]{:S(2)}) %all-to-all-start.2) | async-done | bytes 131104 | tf_op jit(solution)/shard_map/all_to_all | solution.py:542
  85.4 7.1 %backward.3 = (f32[216,256]{1,0:T(8,128)S(1)}, bf16[216,256]{1,0:T(8,128)(2,1)S(1)}, bf16[216,256]{1,0:T(8,128)(2,1)S(1)}, bf16[216,256]{1,0:T(8,128)(2,1)S(1)}) custom-call(s32[4]{0:T(128)S(1)} %and_select_fusion.1.order_ref, bf16[1024,384]{1,0:T(8,128)(2,1)S(1)} %bitcast.11, bf16[4,3072,256]{2,1,0:T(8,128)(2,1)} %get-tuple-element.39.acts_ref, ...), custom_call_target="tpu_custom_call" | custom-call | flops 6000000000 | bytes 18000000 | tf_op jit(solution)/shard_map/backward/pallas_call | solution.py:554
  92.4 3.3 %collective-permute-start.5 = (bf16[216,256]{1,0:T(8,128)(2,1)S(1)}, bf16[216,256]{1,0:T(8,128)(2,1)S(1)}, u32[]{:S(2)}, u32[]{:S(2)}) collective-permute-start(bf16[216,256]{1,0:T(8,128)(2,1)S(1)} %get-tuple-element.41), channel_id=1, source_target_pairs={{0,2},{1,3},{2,0},{3,1},{4,6},{5,7},{6,4},{7,5},{8,10},{9,11},{10,... | collective-permute-start | bytes 331784 | tf_op jit(solution)/shard_map/ppermute | solution.py:551
  95.7 0.7 collective-permute-start.6
  96.4 2.6 %collective-permute-start.7 = (bf16[216,256]{1,0:T(8,128)(2,1)S(1)}, bf16[216,256]{1,0:T(8,128)(2,1)S(1)}, u32[]{:S(2)}, u32[]{:S(2)}) collective-permute-start(bf16[216,256]{1,0:T(8,128)(2,1)S(1)} %get-tuple-element.43), channel_id=1, source_target_pairs={{0,3},{1,0},{2,1},{3,2},{4,7},{5,4},{6,5},{7,6},{8,11},{9,8},{10,9... | collective-permute-start | bytes 331784 | tf_op jit(solution)/shard_map/ppermute | solution.py:551
  98.9 7.1 %backward.2 = (f32[216,256]{1,0:T(8,128)S(1)}, bf16[216,256]{1,0:T(8,128)(2,1)S(1)}, bf16[216,256]{1,0:T(8,128)(2,1)S(1)}, bf16[216,256]{1,0:T(8,128)(2,1)S(1)}) custom-call(s32[4]{0:T(128)S(1)} %and_select_fusion.1.order_ref, bf16[1024,384]{1,0:T(8,128)(2,1)S(1)} %bitcast.12, bf16[4,3072,256]{2,1,0:T(8,128)(2,1)} %get-tuple-element.32.acts_ref, ...), custom_call_target="tpu_custom_call" | custom-call | flops 6000000000 | bytes 18000000 | tf_op jit(solution)/shard_map/backward/pallas_call | solution.py:554
  106.0 0.1 collective-permute-start
  106.1 0.8 collective-permute-start.1
  107.0 0.0 collective-permute-done.5
  107.0 2.5 %collective-permute-start.2 = (bf16[216,256]{1,0:T(8,128)(2,1)S(1)}, bf16[216,256]{1,0:T(8,128)(2,1)S(1)}, u32[]{:S(2)}, u32[]{:S(2)}) collective-permute-start(bf16[216,256]{1,0:T(8,128)(2,1)S(1)} %get-tuple-element.38), channel_id=1, source_target_pairs={{0,3},{1,0},{2,1},{3,2},{4,7},{5,4},{6,5},{7,6},{8,11},{9,8},{10,9... | collective-permute-start | bytes 331784 | tf_op jit(solution)/shard_map/ppermute | solution.py:551
  109.4 0.0 collective-permute-done.6
  109.4 0.0 collective-permute-done.7
  109.4 0.1 add_convert_fusion.refs_3_
  109.5 0.3 collective-permute-start.11
  109.8 3.1 %collective-permute-start.8 = (bf16[216,256]{1,0:T(8,128)(2,1)S(1)}, bf16[216,256]{1,0:T(8,128)(2,1)S(1)}, u32[]{:S(2)}, u32[]{:S(2)}) collective-permute-start(bf16[216,256]{1,0:T(8,128)(2,1)S(1)} %add_convert_fusion.refs_3_), channel_id=1, source_target_pairs={{0,3},{1,0},{2,1},{3,2},{4,7},{5,4},{6,5},{7,6},{8,11},{9,8},{10,9... | collective-permute-start | bytes 331784 | tf_op jit(solution)/shard_map/ppermute | solution.py:551
  112.8 0.8 collective-permute-done
  113.6 1.0 collective-permute-done.1
  114.6 0.0 collective-permute-done.2
  114.6 0.1 add_convert_fusion.1.refs_0_
  114.7 1.2 collective-permute-start.10
  115.9 2.3 %collective-permute-start.3 = (bf16[216,256]{1,0:T(8,128)(2,1)S(1)}, bf16[216,256]{1,0:T(8,128)(2,1)S(1)}, u32[]{:S(2)}, u32[]{:S(2)}) collective-permute-start(bf16[216,256]{1,0:T(8,128)(2,1)S(1)} %add_convert_fusion.1.refs_0_), channel_id=1, source_target_pairs={{0,3},{1,0},{2,1},{3,2},{4,7},{5,4},{6,5},{7,6},{8,11},{9,8},{10,9... | collective-permute-start | bytes 331784 | tf_op jit(solution)/shard_map/ppermute | solution.py:551
  118.2 0.5 and_select_fusion.order_ref
  118.7 0.0 collective-permute-done.8.refs_5_
  118.8 0.2 collective-permute-start.9
  119.0 2.8 %collective-permute-done.3.refs_2_ = bf16[216,256]{1,0:T(8,128)(2,1)S(1)} collective-permute-done((bf16[216,256]{1,0:T(8,128)(2,1)S(1)}, bf16[216,256]{1,0:T(8,128)(2,1)S(1)}, u32[]{:S(2)}, u32[]{:S(2)}) %collective-permute-start.3) | collective-permute-done | bytes 110624 | tf_op jit(solution)/shard_map/ppermute | solution.py:551
  121.7 2.5 %collective-permute-start.4 = (bf16[216,256]{1,0:T(8,128)(2,1)S(1)}, bf16[216,256]{1,0:T(8,128)(2,1)S(1)}, u32[]{:S(2)}, u32[]{:S(2)}) collective-permute-start(bf16[216,256]{1,0:T(8,128)(2,1)S(1)} %collective-permute-done.3.refs_2_), channel_id=1, source_target_pairs={{0,3},{1,0},{2,1},{3,2},{4,7},{5,4},{6,5},{7,6},{8,11},{9,8},{10,9... | collective-permute-start | bytes 331784 | tf_op jit(solution)/shard_map/ppermute | solution.py:551
  124.2 0.0 collective-permute-done.11.refs_4_
  124.2 0.0 collective-permute-done.10.refs_1_
  124.2 0.6 copy-done.14
  124.8 0.6 copy-done.17
  125.5 7.2 %adam.2 = (f32[2,848,256]{2,1,0:T(8,128)}, f32[2,848,256]{2,1,0:T(8,128)}, f32[2,848,256]{2,1,0:T(8,128)}) custom-call(s32[3]{0:T(128)} %and_select_fusion.order_ref, bf16[216,256]{1,0:T(8,128)(2,1)} %copy-done.13, bf16[216,256]{1,0:T(8,128)(2,1)} %copy-done.17, bf16[216,256]{1,0:T(8,128)(2,1)} %copy-done.16, bf16[216,256]{1,0:T(8,128)(2,1)} %copy-done.12, ...), custom_call_target="tpu_custom_call" | custom-call | flops 4000000000 | bytes 12000000 | tf_op jit(solution)/shard_map/adam/pallas_call | solution.py:591
  132.7 0.0 collective-permute-done.9.refs_1_
  132.7 0.0 collective-permute-done.4.refs_0_
  132.7 0.6 copy-done.10
  133.3 0.0 copy-done.11
  133.4 2.6 %adam.3 = (f32[2,848,256]{2,1,0:T(8,128)}, f32[2,848,256]{2,1,0:T(8,128)}, f32[2,848,256]{2,1,0:T(8,128)}) custom-call(s32[1]{0:T(128)S(6)} %select_n.21.order_ref, bf16[216,256]{1,0:T(8,128)(2,1)} %copy-done.11, bf16[216,256]{1,0:T(8,128)(2,1)} %copy-done.10, f32[2,848,256]{2,1,0:T(8,128)} %refs_2_.1, ...), custom_call_target="tpu_custom_call", output_to_operand_aliasing={{0}: (6, {}), {1}: (7, {}), {2}: (8, {})} | custom-call | flops 1500000000 | bytes 4500000 | tf_op jit(solution)/shard_map/adam/pallas_call | solution.py:591
  (29 shorter events, 0.1 us)
Async XLA Ops:
  0.6 42.5 %copy-start = (f32[2,848,256]{2,1,0:T(8,128)S(1)}, f32[2,848,256]{2,1,0:T(8,128)}, u32[]{:S(2)}) copy-start(f32[2,848,256]{2,1,0:T(8,128)} %refs_2_.1) | copy-start | bytes 5210116
  43.1 21.2 %copy-start.1 = (s32[128,32]{0,1:T(8,128)S(1)}, s32[128,32]{0,1:T(8,128)}, u32[]{:S(2)}) copy-start(s32[128,32]{0,1:T(8,128)} %param.19) | copy-start | bytes 49156
  43.1 21.2 %copy-start.2 = (s32[128,32]{0,1:T(8,128)S(1)}, s32[128,32]{0,1:T(8,128)}, u32[]{:S(2)}) copy-start(s32[128,32]{0,1:T(8,128)} %param.20) | copy-start | bytes 49156
  43.1 21.2 %copy-start.3 = (f32[128,32]{0,1:T(8,128)S(1)}, f32[128,32]{0,1:T(8,128)}, u32[]{:S(2)}) copy-start(f32[128,32]{0,1:T(8,128)} %param.16) | copy-start | bytes 49156
  43.1 21.2 %copy-start.4 = (f32[16,64]{1,0:T(8,128)S(1)}, f32[16,64]{1,0:T(8,128)}, u32[]{:S(2)}) copy-start(f32[16,64]{1,0:T(8,128)} %code_ref.1) | copy-start | bytes 12292
  43.1 21.2 %copy-start.5 = (f32[16,64]{1,0:T(8,128)S(1)}, f32[16,64]{1,0:T(8,128)}, u32[]{:S(2)}) copy-start(f32[16,64]{1,0:T(8,128)} %first_ref.1) | copy-start | bytes 12292
  43.1 21.2 %copy-start.6 = (f32[16,64]{1,0:T(8,128)S(1)}, f32[16,64]{1,0:T(8,128)}, u32[]{:S(2)}) copy-start(f32[16,64]{1,0:T(8,128)} %second_ref.1) | copy-start | bytes 12292
  43.1 21.2 %copy-start.7 = (f32[3,128]{1,0:T(4,128)S(1)}, f32[3,128]{1,0:T(4,128)}, u32[]{:S(2)}) copy-start(f32[3,128]{1,0:T(4,128)} %targets_ref.1) | copy-start | bytes 4612
  43.1 21.2 %copy-start.8 = (s32[128]{0:T(128)S(1)}, s32[128]{0:T(128)}, u32[]{:S(2)}) copy-start(s32[128]{0:T(128)} %param.21) | copy-start | bytes 1540
  43.1 21.2 %copy-start.9 = (s32[128]{0:T(128)S(1)}, s32[128]{0:T(128)}, u32[]{:S(2)}) copy-start(s32[128]{0:T(128)} %param.18) | copy-start | bytes 1540
  69.7 15.6 %all-to-all-start.2 = ((bf16[64,8,128]{2,1,0:T(8,128)(2,1)}), bf16[64,8,128]{2,1,0:T(8,128)(2,1)S(1)}, u32[]{:S(2)}, u32[]{:S(2)}) async-start(bf16[64,8,128]{2,1,0:T(8,128)(2,1)} %get-tuple-element.33), calls=%async_computation.2 | async-start | bytes 262144 | tf_op jit(solution)/shard_map/all_to_all | solution.py:542
  92.4 14.5 %collective-permute-start.5 = (bf16[216,256]{1,0:T(8,128)(2,1)S(1)}, bf16[216,256]{1,0:T(8,128)(2,1)S(1)}, u32[]{:S(2)}, u32[]{:S(2)}) collective-permute-start(bf16[216,256]{1,0:T(8,128)(2,1)S(1)} %get-tuple-element.41), channel_id=1, source_target_pairs={{0,2},{1,3},{2,0},{3,1},{4,6},{5,7},{6,4},{7,5},{8,10},{9,11},{10,... | collective-permute-start | bytes 331784 | tf_op jit(solution)/shard_map/ppermute | solution.py:551
  95.7 13.7 %collective-permute-start.6 = (bf16[216,256]{1,0:T(8,128)(2,1)S(1)}, bf16[216,256]{1,0:T(8,128)(2,1)S(1)}, u32[]{:S(2)}, u32[]{:S(2)}) collective-permute-start(bf16[216,256]{1,0:T(8,128)(2,1)S(1)} %get-tuple-element.42), channel_id=1, source_target_pairs={{0,1},{1,2},{2,3},{3,0},{4,5},{5,6},{6,7},{7,4},{8,9},{9,10},{10,1... | collective-permute-start | bytes 331784 | tf_op jit(solution)/shard_map/ppermute | solution.py:551
  96.4 13.1 %collective-permute-start.7 = (bf16[216,256]{1,0:T(8,128)(2,1)S(1)}, bf16[216,256]{1,0:T(8,128)(2,1)S(1)}, u32[]{:S(2)}, u32[]{:S(2)}) collective-permute-start(bf16[216,256]{1,0:T(8,128)(2,1)S(1)} %get-tuple-element.43), channel_id=1, source_target_pairs={{0,3},{1,0},{2,1},{3,2},{4,7},{5,4},{6,5},{7,6},{8,11},{9,8},{10,9... | collective-permute-start | bytes 331784 | tf_op jit(solution)/shard_map/ppermute | solution.py:551
  98.9 19.3 %copy-start.18 = (s32[3]{0:T(128)S(1)}, s32[3]{0:T(128)}, u32[]{:S(2)}) copy-start(s32[3]{0:T(128)} %constant.49.clone) | copy-start | bytes 40
  106.0 7.6 %collective-permute-start = (bf16[216,256]{1,0:T(8,128)(2,1)S(1)}, bf16[216,256]{1,0:T(8,128)(2,1)S(1)}, u32[]{:S(2)}, u32[]{:S(2)}) collective-permute-start(bf16[216,256]{1,0:T(8,128)(2,1)S(1)} %get-tuple-element.36), channel_id=1, source_target_pairs={{0,2},{1,3},{2,0},{3,1},{4,6},{5,7},{6,4},{7,5},{8,10},{9,11},{10,... | collective-permute-start | bytes 331784 | tf_op jit(solution)/shard_map/ppermute | solution.py:551
  106.1 8.5 %collective-permute-start.1 = (bf16[216,256]{1,0:T(8,128)(2,1)S(1)}, bf16[216,256]{1,0:T(8,128)(2,1)S(1)}, u32[]{:S(2)}, u32[]{:S(2)}) collective-permute-start(bf16[216,256]{1,0:T(8,128)(2,1)S(1)} %get-tuple-element.37), channel_id=1, source_target_pairs={{0,1},{1,2},{2,3},{3,0},{4,5},{5,6},{6,7},{7,4},{8,9},{9,10},{10,1... | collective-permute-start | bytes 331784 | tf_op jit(solution)/shard_map/ppermute | solution.py:551
  107.0 7.6 %collective-permute-start.2 = (bf16[216,256]{1,0:T(8,128)(2,1)S(1)}, bf16[216,256]{1,0:T(8,128)(2,1)S(1)}, u32[]{:S(2)}, u32[]{:S(2)}) collective-permute-start(bf16[216,256]{1,0:T(8,128)(2,1)S(1)} %get-tuple-element.38), channel_id=1, source_target_pairs={{0,3},{1,0},{2,1},{3,2},{4,7},{5,4},{6,5},{7,6},{8,11},{9,8},{10,9... | collective-permute-start | bytes 331784 | tf_op jit(solution)/shard_map/ppermute | solution.py:551
  109.5 14.7 %copy-start.12 = (bf16[216,256]{1,0:T(8,128)(2,1)}, bf16[216,256]{1,0:T(8,128)(2,1)S(1)}, u32[]{:S(2)}) copy-start(bf16[216,256]{1,0:T(8,128)(2,1)S(1)} %add_convert_fusion.refs_3_) | copy-start | bytes 331780
  109.5 14.6 %collective-permute-start.11 = (bf16[216,256]{1,0:T(8,128)(2,1)S(1)}, bf16[216,256]{1,0:T(8,128)(2,1)S(1)}, u32[]{:S(2)}, u32[]{:S(2)}) collective-permute-start(bf16[216,256]{1,0:T(8,128)(2,1)S(1)} %add_convert_fusion.refs_3_), channel_id=1, source_target_pairs={{0,1},{1,2},{2,3},{3,0},{4,5},{5,6},{6,7},{7,4},{8,9},{9,10},{10,1... | collective-permute-start | bytes 331784 | tf_op jit(solution)/shard_map/ppermute | solution.py:551
  109.8 9.0 %collective-permute-start.8 = (bf16[216,256]{1,0:T(8,128)(2,1)S(1)}, bf16[216,256]{1,0:T(8,128)(2,1)S(1)}, u32[]{:S(2)}, u32[]{:S(2)}) collective-permute-start(bf16[216,256]{1,0:T(8,128)(2,1)S(1)} %add_convert_fusion.refs_3_), channel_id=1, source_target_pairs={{0,3},{1,0},{2,1},{3,2},{4,7},{5,4},{6,5},{7,6},{8,11},{9,8},{10,9... | collective-permute-start | bytes 331784 | tf_op jit(solution)/shard_map/ppermute | solution.py:551
  114.7 9.5 %copy-start.13 = (bf16[216,256]{1,0:T(8,128)(2,1)}, bf16[216,256]{1,0:T(8,128)(2,1)S(1)}, u32[]{:S(2)}) copy-start(bf16[216,256]{1,0:T(8,128)(2,1)S(1)} %add_convert_fusion.1.refs_0_) | copy-start | bytes 331780
  114.7 9.5 %collective-permute-start.10 = (bf16[216,256]{1,0:T(8,128)(2,1)S(1)}, bf16[216,256]{1,0:T(8,128)(2,1)S(1)}, u32[]{:S(2)}, u32[]{:S(2)}) collective-permute-start(bf16[216,256]{1,0:T(8,128)(2,1)S(1)} %add_convert_fusion.1.refs_0_), channel_id=1, source_target_pairs={{0,1},{1,2},{2,3},{3,0},{4,5},{5,6},{6,7},{7,4},{8,9},{9,10},{10,1... | collective-permute-start | bytes 331784 | tf_op jit(solution)/shard_map/ppermute | solution.py:551
  115.9 5.8 %collective-permute-start.3 = (bf16[216,256]{1,0:T(8,128)(2,1)S(1)}, bf16[216,256]{1,0:T(8,128)(2,1)S(1)}, u32[]{:S(2)}, u32[]{:S(2)}) collective-permute-start(bf16[216,256]{1,0:T(8,128)(2,1)S(1)} %add_convert_fusion.1.refs_0_), channel_id=1, source_target_pairs={{0,3},{1,0},{2,1},{3,2},{4,7},{5,4},{6,5},{7,6},{8,11},{9,8},{10,9... | collective-permute-start | bytes 331784 | tf_op jit(solution)/shard_map/ppermute | solution.py:551
  118.7 5.5 %copy-start.15 = (bf16[216,256]{1,0:T(8,128)(2,1)}, bf16[216,256]{1,0:T(8,128)(2,1)S(1)}, u32[]{:S(2)}) copy-start(bf16[216,256]{1,0:T(8,128)(2,1)S(1)} %collective-permute-done.8.refs_5_) | copy-start | bytes 331780
  118.8 13.9 %collective-permute-start.9 = (bf16[216,256]{1,0:T(8,128)(2,1)S(1)}, bf16[216,256]{1,0:T(8,128)(2,1)S(1)}, u32[]{:S(2)}, u32[]{:S(2)}) collective-permute-start(bf16[216,256]{1,0:T(8,128)(2,1)S(1)} %collective-permute-done.8.refs_5_), channel_id=1, source_target_pairs={{0,3},{1,0},{2,1},{3,2},{4,7},{5,4},{6,5},{7,6},{8,11},{9,8},{10,9... | collective-permute-start | bytes 331784 | tf_op jit(solution)/shard_map/ppermute | solution.py:551
  121.7 2.5 %copy-start.16 = (bf16[216,256]{1,0:T(8,128)(2,1)}, bf16[216,256]{1,0:T(8,128)(2,1)S(1)}, u32[]{:S(2)}) copy-start(bf16[216,256]{1,0:T(8,128)(2,1)S(1)} %collective-permute-done.3.refs_2_) | copy-start | bytes 331780
  121.7 11.0 %collective-permute-start.4 = (bf16[216,256]{1,0:T(8,128)(2,1)S(1)}, bf16[216,256]{1,0:T(8,128)(2,1)S(1)}, u32[]{:S(2)}, u32[]{:S(2)}) collective-permute-start(bf16[216,256]{1,0:T(8,128)(2,1)S(1)} %collective-permute-done.3.refs_2_), channel_id=1, source_target_pairs={{0,3},{1,0},{2,1},{3,2},{4,7},{5,4},{6,5},{7,6},{8,11},{9,8},{10,9... | collective-permute-start | bytes 331784 | tf_op jit(solution)/shard_map/ppermute | solution.py:551
  124.2 0.6 copy-start.14
  124.8 0.6 copy-start.17
  132.7 0.6 copy-start.10
  132.7 0.7 copy-start.11

commit v3 on v0

--- a/solution.py
+++ b/solution.py
@@ -584,13 +584,14 @@
             name="backward",
         )((position + turns) % copies, arrived, acts[h], cot_in, weights)
 
-    def collect(shares):
+    def collect(shares, forwarded):
         share = shares[0]
         for k in (2, 1, 3):
             share = share + send(shares[k], k).astype(F32)
         share = share.astype(BF16)
         behind, ahead = send(share, 1), send(share, 3)
-        return share, behind, send(ahead, 3), ahead
+        far = send(ahead, 3) if forwarded else send(share, 2)
+        return share, behind, far, ahead
 
     def update(h, pieces, earlier):
         block = pl.BlockSpec((1, quarter, NET_WIDTH), lambda i, order: (h, order[i], 0))
@@ -618,7 +619,7 @@
             *earlier,
         )
 
-    pieces = [collect(gradient(h)) for h in range(2)]
+    pieces = [collect(gradient(h), h == 1) for h in range(2)]
     updated = update(0, pieces[0], ())
     new_params, new_first, new_second = update(1, pieces[1], updated)
     return (

time: 130 us -> 130 us (level)
  waiting for transfers between devices: 14.4 us -> 16.3 us
  starting transfers between devices: 24 us -> 22.3 us
    ppermute x12, waiting for transfers between devices: 4.41 us -> 6.28 us  [send(): lax.ppermute(value, 'dp', [(i, (i + distance) % copies) for i in range(co...]
    ppermute x12, starting transfers between devices: 18.4 us -> 16.7 us  [send(): lax.ppermute(value, 'dp', [(i, (i + distance) % copies) for i in range(co...]
where the time goes in v3:
time: 130 us; the launch traced here: 129 us
  blocking collectives  50.8 us (39%)
  Pallas kernels  38.4 us (30%)
  starting transfers between devices  22.3 us (17%)
  waiting for transfers between devices  16.3 us (13%)
    all_to_all x1, blocking collectives, shards(): lax.all_to_all(outgoing, 'expert', split_axis=0, concat_axis=0, tiled=True)  35.2 us
    ppermute x12, starting transfers between devices, send(): lax.ppermute(value, 'dp', [(i, (i + distance) % copies) for i in range(co...  16.7 us
    all_to_all x1, blocking collectives, shards(): lax.all_to_all(raw_out, 'expert', split_axis=0, concat_axis=0, tiled=True)  15.6 us
    pallas_call x2, Pallas kernels, gradient(): pl.pallas_call(functools.partial(backward_kernel, h), grid_spec=pltpu.Pre...  14.4 us
    all_to_all x1, waiting for transfers between devices, shards(): lax.all_to_all(cot_out, 'expert', split_axis=0, concat_axis=0, tiled=True)  9.98 us
    pallas_call x1, Pallas kernels, shards(): pl.pallas_call(dispatch_kernel, out_shape=shape_of((places, THIRDS * 128)...  7.21 us
    ppermute x12, waiting for transfers between devices, send(): lax.ppermute(value, 'dp', [(i, (i + distance) % copies) for i in range(co...  6.28 us
    pallas_call x2, Pallas kernels, update(): pl.pallas_call(adam_kernel, grid_spec=pltpu.PrefetchScalarGridSpec(num_sc...  5.79 us
  transfers between devices with their start and end apart: 13, of which 4 were waited for; matrix products, arithmetic and copies ran while one was open for 0% of the time, Pallas kernels for 8%

profile of v3, /device:TPU:2, one launch (start us, length us, event | category | flops | bytes accessed | tf_op | source)
XLA Modules:
  0.0 128.8 jit_solution(14260297447895941821)
XLA Ops:
  0.6 7.2 %dispatch.1 = bf16[1024,384]{1,0:T(8,128)(2,1)} custom-call(bf16[32,64,128]{2,1,0:T(8,128)(2,1)} %bitcast.20, s32[32,128]{1,0:T(8,128)} %bitcast.12, s32[32,128]{1,0:T(8,128)} %bitcast.14), custom_call_target="tpu_custom_call" | custom-call | tf_op jit(solution)/shard_map/dispatch/pallas_call | solution.py:482
  7.9 35.2 %all_to_all.21 = bf16[64,16,384]{2,1,0:T(8,128)(2,1)S(1)} all-to-all(bf16[64,16,384]{2,1,0:T(8,128)(2,1)} %bitcast.19), channel_id=1, replica_groups=mesh['expert'=64,'dp'=4] {'expert'}, dimensions={0} | all-to-all | bytes 1572864 | tf_op jit(solution)/shard_map/all_to_all | solution.py:497
  43.1 0.0 copy-start.7
  43.1 0.0 copy-start.8
  43.1 0.0 copy-start.9
  43.1 0.0 copy-start.10
  43.1 0.0 copy-start.11
  43.1 0.0 copy-done
  43.1 5.5 %forward.1 = (bf16[4,3072,256]{2,1,0:T(8,128)(2,1)}, bf16[4,3072,256]{2,1,0:T(8,128)(2,1)}, bf16[64,8,128]{2,1,0:T(8,128)(2,1)S(1)}, bf16[2,848,256]{2,1,0:T(8,128)(2,1)S(1)}) custom-call(bf16[1024,384]{1,0:T(8,128)(2,1)S(1)} %bitcast.9, f32[2,848,256]{2,1,0:T(8,128)S(1)} %copy-done), custom_call_target="tpu_custom_call" | custom-call | tf_op jit(solution)/shard_map/forward/pallas_call | solution.py:503
  48.7 15.6 %all_to_all.22.back_ref = bf16[64,8,128]{2,1,0:T(8,128)(2,1)S(1)} all-to-all(bf16[64,8,128]{2,1,0:T(8,128)(2,1)S(1)} %get-tuple-element.30), channel_id=1, replica_groups=mesh['expert'=64,'dp'=4] {'expert'}, dimensions={0} | all-to-all | bytes 262144 | tf_op jit(solution)/shard_map/all_to_all | solution.py:520
  64.3 0.0 copy-done.5
  64.3 0.0 copy-done.6
  64.3 0.0 copy-done.7
  64.3 0.0 copy-done.8
  64.3 0.0 copy-done.9
  64.3 5.4 %rays.1 = (bf16[64,8,128]{2,1,0:T(8,128)(2,1)}, f32[1,128]{1,0:T(1,128)}, f32[16,64]{1,0:T(8,128)}, f32[16,64]{1,0:T(8,128)}, f32[16,64]{1,0:T(8,128)}) custom-call(bf16[64,8,128]{2,1,0:T(8,128)(2,1)S(1)} %all_to_all.22.back_ref, s32[32,128]{1,0:T(8,128)S(1)} %bitcast.13, s32[32,128]{1,0:T(8,128)S(1)} %bitcast.15, s32[1,128]{1,0:T(1,128)S(1)} %bitcast.17, ...), custom_call_target="tpu_custom_call" | custom-call | tf_op jit(solution)/shard_map/rays/pallas_call | solution.py:523
  69.7 5.6 %all-to-all-start.2 = ((bf16[64,8,128]{2,1,0:T(8,128)(2,1)}), bf16[64,8,128]{2,1,0:T(8,128)(2,1)S(1)}, u32[]{:S(2)}, u32[]{:S(2)}) async-start(bf16[64,8,128]{2,1,0:T(8,128)(2,1)} %get-tuple-element.33), calls=%async_computation.2 | async-start | bytes 262144 | tf_op jit(solution)/shard_map/all_to_all | solution.py:551
  75.4 10.0 %all-to-all-done.2.cot_in_ref = bf16[64,8,128]{2,1,0:T(8,128)(2,1)S(1)} async-done(((bf16[64,8,128]{2,1,0:T(8,128)(2,1)}), bf16[64,8,128]{2,1,0:T(8,128)(2,1)S(1)}, u32[]{:S(2)}, u32[]{:S(2)}) %all-to-all-start.2) | async-done | bytes 131104 | tf_op jit(solution)/shard_map/all_to_all | solution.py:551
  85.4 7.1 %backward.3 = (f32[216,256]{1,0:T(8,128)S(1)}, bf16[216,256]{1,0:T(8,128)(2,1)S(1)}, bf16[216,256]{1,0:T(8,128)(2,1)S(1)}, bf16[216,256]{1,0:T(8,128)(2,1)S(1)}) custom-call(s32[4]{0:T(128)S(1)} %and_select_fusion.order_ref, bf16[1024,384]{1,0:T(8,128)(2,1)S(1)} %bitcast.10, bf16[4,3072,256]{2,1,0:T(8,128)(2,1)} %get-tuple-element.39.acts_ref, ...), custom_call_target="tpu_custom_call" | custom-call | flops 6000000000 | bytes 18000000 | tf_op jit(solution)/shard_map/backward/pallas_call | solution.py:563
  92.4 3.3 %collective-permute-start.6 = (bf16[216,256]{1,0:T(8,128)(2,1)S(1)}, bf16[216,256]{1,0:T(8,128)(2,1)S(1)}, u32[]{:S(2)}, u32[]{:S(2)}) collective-permute-start(bf16[216,256]{1,0:T(8,128)(2,1)S(1)} %get-tuple-element.41), channel_id=1, source_target_pairs={{0,2},{1,3},{2,0},{3,1},{4,6},{5,7},{6,4},{7,5},{8,10},{9,11},{10,... | collective-permute-start | bytes 331784 | tf_op jit(solution)/shard_map/ppermute | solution.py:560
  95.7 0.7 collective-permute-start.7
  96.4 2.6 %collective-permute-start.8 = (bf16[216,256]{1,0:T(8,128)(2,1)S(1)}, bf16[216,256]{1,0:T(8,128)(2,1)S(1)}, u32[]{:S(2)}, u32[]{:S(2)}) collective-permute-start(bf16[216,256]{1,0:T(8,128)(2,1)S(1)} %get-tuple-element.43), channel_id=1, source_target_pairs={{0,3},{1,0},{2,1},{3,2},{4,7},{5,4},{6,5},{7,6},{8,11},{9,8},{10,9... | collective-permute-start | bytes 331784 | tf_op jit(solution)/shard_map/ppermute | solution.py:560
  98.9 7.4 %backward.2 = (f32[216,256]{1,0:T(8,128)S(1)}, bf16[216,256]{1,0:T(8,128)(2,1)S(1)}, bf16[216,256]{1,0:T(8,128)(2,1)S(1)}, bf16[216,256]{1,0:T(8,128)(2,1)S(1)}) custom-call(s32[4]{0:T(128)S(1)} %and_select_fusion.order_ref, bf16[1024,384]{1,0:T(8,128)(2,1)S(1)} %bitcast.11, bf16[4,3072,256]{2,1,0:T(8,128)(2,1)} %get-tuple-element.32.acts_ref, ...), custom_call_target="tpu_custom_call" | custom-call | flops 6000000000 | bytes 18000000 | tf_op jit(solution)/shard_map/backward/pallas_call | solution.py:563
  106.3 0.1 collective-permute-start
  106.4 0.8 collective-permute-start.1
  107.3 0.0 collective-permute-done.6
  107.3 2.5 %collective-permute-start.2 = (bf16[216,256]{1,0:T(8,128)(2,1)S(1)}, bf16[216,256]{1,0:T(8,128)(2,1)S(1)}, u32[]{:S(2)}, u32[]{:S(2)}) collective-permute-start(bf16[216,256]{1,0:T(8,128)(2,1)S(1)} %get-tuple-element.38), channel_id=1, source_target_pairs={{0,3},{1,0},{2,1},{3,2},{4,7},{5,4},{6,5},{7,6},{8,11},{9,8},{10,9... | collective-permute-start | bytes 331784 | tf_op jit(solution)/shard_map/ppermute | solution.py:560
  109.7 0.0 collective-permute-done.7
  109.7 0.0 collective-permute-done.8
  109.7 0.1 add_convert_fusion.own_ref
  109.8 0.9 collective-permute-start.11
  110.7 1.5 %collective-permute-start.10 = (bf16[216,256]{1,0:T(8,128)(2,1)S(1)}, bf16[216,256]{1,0:T(8,128)(2,1)S(1)}, u32[]{:S(2)}, u32[]{:S(2)}) collective-permute-start(bf16[216,256]{1,0:T(8,128)(2,1)S(1)} %add_convert_fusion.own_ref), channel_id=1, source_target_pairs={{0,2},{1,3},{2,0},{3,1},{4,6},{5,7},{6,4},{7,5},{8,10},{9,11},{10,... | collective-permute-start | bytes 331784 | tf_op jit(solution)/shard_map/ppermute | solution.py:560
  112.2 1.3 %collective-permute-done = bf16[216,256]{1,0:T(8,128)(2,1)S(1)} collective-permute-done((bf16[216,256]{1,0:T(8,128)(2,1)S(1)}, bf16[216,256]{1,0:T(8,128)(2,1)S(1)}, u32[]{:S(2)}, u32[]{:S(2)}) %collective-permute-start) | collective-permute-done | bytes 110624 | tf_op jit(solution)/shard_map/ppermute | solution.py:560
  113.5 0.0 collective-permute-start.9
  113.5 2.2 %collective-permute-done.1 = bf16[216,256]{1,0:T(8,128)(2,1)S(1)} collective-permute-done((bf16[216,256]{1,0:T(8,128)(2,1)S(1)}, bf16[216,256]{1,0:T(8,128)(2,1)S(1)}, u32[]{:S(2)}, u32[]{:S(2)}) %collective-permute-start.1) | collective-permute-done | bytes 110624 | tf_op jit(solution)/shard_map/ppermute | solution.py:560
  115.8 0.0 collective-permute-done.2
  115.8 0.1 add_convert_fusion.1.own_ref
  115.8 1.2 collective-permute-start.4
  117.0 0.9 collective-permute-start.3
  117.9 2.7 %collective-permute-done.4.third_ref = bf16[216,256]{1,0:T(8,128)(2,1)S(1)} collective-permute-done((bf16[216,256]{1,0:T(8,128)(2,1)S(1)}, bf16[216,256]{1,0:T(8,128)(2,1)S(1)}, u32[]{:S(2)}, u32[]{:S(2)}) %collective-permute-start.4) | collective-permute-done | bytes 110624 | tf_op jit(solution)/shard_map/ppermute | solution.py:560
  120.7 2.3 %collective-permute-start.5 = (bf16[216,256]{1,0:T(8,128)(2,1)S(1)}, bf16[216,256]{1,0:T(8,128)(2,1)S(1)}, u32[]{:S(2)}, u32[]{:S(2)}) collective-permute-start(bf16[216,256]{1,0:T(8,128)(2,1)S(1)} %collective-permute-done.4.third_ref), channel_id=1, source_target_pairs={{0,3},{1,0},{2,1},{3,2},{4,7},{5,4},{6,5},{7,6},{8,11},{9,8},{10,9... | collective-permute-start | bytes 331784 | tf_op jit(solution)/shard_map/ppermute | solution.py:560
  123.0 0.0 collective-permute-done.11.third_ref
  123.0 0.0 collective-permute-done.10.second_ref
  123.0 0.0 collective-permute-done.9.first_ref
  123.0 2.9 %adam.2 = (f32[2,848,256]{2,1,0:T(8,128)}, f32[2,848,256]{2,1,0:T(8,128)}, f32[2,848,256]{2,1,0:T(8,128)}) custom-call(s32[4]{0:T(128)S(1)} %and_select_fusion.1.order_ref, bf16[216,256]{1,0:T(8,128)(2,1)S(1)} %add_convert_fusion.own_ref, bf16[216,256]{1,0:T(8,128)(2,1)S(1)} %collective-permute-done.9.first_ref, ...), custom_call_target="tpu_custom_call" | custom-call | flops 2000000000 | bytes 6000000 | tf_op jit(solution)/shard_map/adam/pallas_call | solution.py:598
  125.9 0.0 collective-permute-done.3.first_ref
  125.9 0.0 collective-permute-done.5.second_ref
  125.9 2.9 %adam.3 = (f32[2,848,256]{2,1,0:T(8,128)}, f32[2,848,256]{2,1,0:T(8,128)}, f32[2,848,256]{2,1,0:T(8,128)}) custom-call(s32[4]{0:T(128)S(1)} %and_select_fusion.1.order_ref, bf16[216,256]{1,0:T(8,128)(2,1)S(1)} %add_convert_fusion.1.own_ref, ...), custom_call_target="tpu_custom_call", output_to_operand_aliasing={{0}: (8, {}), {1}: (9, {}), {2}: (10, {})} | custom-call | flops 2000000000 | bytes 6000000 | tf_op jit(solution)/shard_map/adam/pallas_call | solution.py:598
  (15 shorter events, 0.0 us)
Async XLA Ops:
  0.6 42.5 %copy-start = (f32[2,848,256]{2,1,0:T(8,128)S(1)}, f32[2,848,256]{2,1,0:T(8,128)}, u32[]{:S(2)}) copy-start(f32[2,848,256]{2,1,0:T(8,128)} %param_ref.3) | copy-start | bytes 5210116
  43.1 21.2 %copy-start.3 = (s32[128,32]{0,1:T(8,128)S(1)}, s32[128,32]{0,1:T(8,128)}, u32[]{:S(2)}) copy-start(s32[128,32]{0,1:T(8,128)} %param.17) | copy-start | bytes 49156
  43.1 21.2 %copy-start.4 = (s32[128,32]{0,1:T(8,128)S(1)}, s32[128,32]{0,1:T(8,128)}, u32[]{:S(2)}) copy-start(s32[128,32]{0,1:T(8,128)} %param.18) | copy-start | bytes 49156
  43.1 21.2 %copy-start.5 = (f32[128,32]{0,1:T(8,128)S(1)}, f32[128,32]{0,1:T(8,128)}, u32[]{:S(2)}) copy-start(f32[128,32]{0,1:T(8,128)} %param.14) | copy-start | bytes 49156
  43.1 21.2 %copy-start.6 = (f32[16,64]{1,0:T(8,128)S(1)}, f32[16,64]{1,0:T(8,128)}, u32[]{:S(2)}) copy-start(f32[16,64]{1,0:T(8,128)} %code_ref.1) | copy-start | bytes 12292
  43.1 21.2 %copy-start.7 = (f32[16,64]{1,0:T(8,128)S(1)}, f32[16,64]{1,0:T(8,128)}, u32[]{:S(2)}) copy-start(f32[16,64]{1,0:T(8,128)} %first_ref.1) | copy-start | bytes 12292
  43.1 21.2 %copy-start.8 = (f32[16,64]{1,0:T(8,128)S(1)}, f32[16,64]{1,0:T(8,128)}, u32[]{:S(2)}) copy-start(f32[16,64]{1,0:T(8,128)} %second_ref.1) | copy-start | bytes 12292
  43.1 21.2 %copy-start.9 = (f32[3,128]{1,0:T(4,128)S(1)}, f32[3,128]{1,0:T(4,128)}, u32[]{:S(2)}) copy-start(f32[3,128]{1,0:T(4,128)} %targets_ref.1) | copy-start | bytes 4612
  43.1 21.2 %copy-start.10 = (s32[128]{0:T(128)S(1)}, s32[128]{0:T(128)}, u32[]{:S(2)}) copy-start(s32[128]{0:T(128)} %param.19) | copy-start | bytes 1540
  43.1 21.2 %copy-start.11 = (s32[128]{0:T(128)S(1)}, s32[128]{0:T(128)}, u32[]{:S(2)}) copy-start(s32[128]{0:T(128)} %param.16) | copy-start | bytes 1540
  69.7 15.6 %all-to-all-start.2 = ((bf16[64,8,128]{2,1,0:T(8,128)(2,1)}), bf16[64,8,128]{2,1,0:T(8,128)(2,1)S(1)}, u32[]{:S(2)}, u32[]{:S(2)}) async-start(bf16[64,8,128]{2,1,0:T(8,128)(2,1)} %get-tuple-element.33), calls=%async_computation.2 | async-start | bytes 262144 | tf_op jit(solution)/shard_map/all_to_all | solution.py:551
  92.4 14.8 %collective-permute-start.6 = (bf16[216,256]{1,0:T(8,128)(2,1)S(1)}, bf16[216,256]{1,0:T(8,128)(2,1)S(1)}, u32[]{:S(2)}, u32[]{:S(2)}) collective-permute-start(bf16[216,256]{1,0:T(8,128)(2,1)S(1)} %get-tuple-element.41), channel_id=1, source_target_pairs={{0,2},{1,3},{2,0},{3,1},{4,6},{5,7},{6,4},{7,5},{8,10},{9,11},{10,... | collective-permute-start | bytes 331784 | tf_op jit(solution)/shard_map/ppermute | solution.py:560
  95.7 14.0 %collective-permute-start.7 = (bf16[216,256]{1,0:T(8,128)(2,1)S(1)}, bf16[216,256]{1,0:T(8,128)(2,1)S(1)}, u32[]{:S(2)}, u32[]{:S(2)}) collective-permute-start(bf16[216,256]{1,0:T(8,128)(2,1)S(1)} %get-tuple-element.42), channel_id=1, source_target_pairs={{0,1},{1,2},{2,3},{3,0},{4,5},{5,6},{6,7},{7,4},{8,9},{9,10},{10,1... | collective-permute-start | bytes 331784 | tf_op jit(solution)/shard_map/ppermute | solution.py:560
  96.4 13.4 %collective-permute-start.8 = (bf16[216,256]{1,0:T(8,128)(2,1)S(1)}, bf16[216,256]{1,0:T(8,128)(2,1)S(1)}, u32[]{:S(2)}, u32[]{:S(2)}) collective-permute-start(bf16[216,256]{1,0:T(8,128)(2,1)S(1)} %get-tuple-element.43), channel_id=1, source_target_pairs={{0,3},{1,0},{2,1},{3,2},{4,7},{5,4},{6,5},{7,6},{8,11},{9,8},{10,9... | collective-permute-start | bytes 331784 | tf_op jit(solution)/shard_map/ppermute | solution.py:560
  98.9 24.0 %copy-start.1 = (f32[2,848,256]{2,1,0:T(8,128)S(1)}, f32[2,848,256]{2,1,0:T(8,128)}, u32[]{:S(2)}) copy-start(f32[2,848,256]{2,1,0:T(8,128)} %one_ref.3) | copy-start | bytes 5210116
  98.9 24.1 %copy-start.2 = (f32[2,848,256]{2,1,0:T(8,128)S(1)}, f32[2,848,256]{2,1,0:T(8,128)}, u32[]{:S(2)}) copy-start(f32[2,848,256]{2,1,0:T(8,128)} %two_ref.3) | copy-start | bytes 5210116
  106.3 7.2 %collective-permute-start = (bf16[216,256]{1,0:T(8,128)(2,1)S(1)}, bf16[216,256]{1,0:T(8,128)(2,1)S(1)}, u32[]{:S(2)}, u32[]{:S(2)}) collective-permute-start(bf16[216,256]{1,0:T(8,128)(2,1)S(1)} %get-tuple-element.36), channel_id=1, source_target_pairs={{0,2},{1,3},{2,0},{3,1},{4,6},{5,7},{6,4},{7,5},{8,10},{9,11},{10,... | collective-permute-start | bytes 331784 | tf_op jit(solution)/shard_map/ppermute | solution.py:560
  106.4 9.4 %collective-permute-start.1 = (bf16[216,256]{1,0:T(8,128)(2,1)S(1)}, bf16[216,256]{1,0:T(8,128)(2,1)S(1)}, u32[]{:S(2)}, u32[]{:S(2)}) collective-permute-start(bf16[216,256]{1,0:T(8,128)(2,1)S(1)} %get-tuple-element.37), channel_id=1, source_target_pairs={{0,1},{1,2},{2,3},{3,0},{4,5},{5,6},{6,7},{7,4},{8,9},{9,10},{10,1... | collective-permute-start | bytes 331784 | tf_op jit(solution)/shard_map/ppermute | solution.py:560
  107.3 8.5 %collective-permute-start.2 = (bf16[216,256]{1,0:T(8,128)(2,1)S(1)}, bf16[216,256]{1,0:T(8,128)(2,1)S(1)}, u32[]{:S(2)}, u32[]{:S(2)}) collective-permute-start(bf16[216,256]{1,0:T(8,128)(2,1)S(1)} %get-tuple-element.38), channel_id=1, source_target_pairs={{0,3},{1,0},{2,1},{3,2},{4,7},{5,4},{6,5},{7,6},{8,11},{9,8},{10,9... | collective-permute-start | bytes 331784 | tf_op jit(solution)/shard_map/ppermute | solution.py:560
  109.8 13.2 %collective-permute-start.11 = (bf16[216,256]{1,0:T(8,128)(2,1)S(1)}, bf16[216,256]{1,0:T(8,128)(2,1)S(1)}, u32[]{:S(2)}, u32[]{:S(2)}) collective-permute-start(bf16[216,256]{1,0:T(8,128)(2,1)S(1)} %add_convert_fusion.own_ref), channel_id=1, source_target_pairs={{0,3},{1,0},{2,1},{3,2},{4,7},{5,4},{6,5},{7,6},{8,11},{9,8},{10,9... | collective-permute-start | bytes 331784 | tf_op jit(solution)/shard_map/ppermute | solution.py:560
  110.7 12.3 %collective-permute-start.10 = (bf16[216,256]{1,0:T(8,128)(2,1)S(1)}, bf16[216,256]{1,0:T(8,128)(2,1)S(1)}, u32[]{:S(2)}, u32[]{:S(2)}) collective-permute-start(bf16[216,256]{1,0:T(8,128)(2,1)S(1)} %add_convert_fusion.own_ref), channel_id=1, source_target_pairs={{0,2},{1,3},{2,0},{3,1},{4,6},{5,7},{6,4},{7,5},{8,10},{9,11},{10,... | collective-permute-start | bytes 331784 | tf_op jit(solution)/shard_map/ppermute | solution.py:560
  113.5 9.4 %collective-permute-start.9 = (bf16[216,256]{1,0:T(8,128)(2,1)S(1)}, bf16[216,256]{1,0:T(8,128)(2,1)S(1)}, u32[]{:S(2)}, u32[]{:S(2)}) collective-permute-start(bf16[216,256]{1,0:T(8,128)(2,1)S(1)} %add_convert_fusion.own_ref), channel_id=1, source_target_pairs={{0,1},{1,2},{2,3},{3,0},{4,5},{5,6},{6,7},{7,4},{8,9},{9,10},{10,1... | collective-permute-start | bytes 331784 | tf_op jit(solution)/shard_map/ppermute | solution.py:560
  115.8 4.8 %collective-permute-start.4 = (bf16[216,256]{1,0:T(8,128)(2,1)S(1)}, bf16[216,256]{1,0:T(8,128)(2,1)S(1)}, u32[]{:S(2)}, u32[]{:S(2)}) collective-permute-start(bf16[216,256]{1,0:T(8,128)(2,1)S(1)} %add_convert_fusion.1.own_ref), channel_id=1, source_target_pairs={{0,3},{1,0},{2,1},{3,2},{4,7},{5,4},{6,5},{7,6},{8,11},{9,8},{10,9... | collective-permute-start | bytes 331784 | tf_op jit(solution)/shard_map/ppermute | solution.py:560
  117.0 8.9 %collective-permute-start.3 = (bf16[216,256]{1,0:T(8,128)(2,1)S(1)}, bf16[216,256]{1,0:T(8,128)(2,1)S(1)}, u32[]{:S(2)}, u32[]{:S(2)}) collective-permute-start(bf16[216,256]{1,0:T(8,128)(2,1)S(1)} %add_convert_fusion.1.own_ref), channel_id=1, source_target_pairs={{0,1},{1,2},{2,3},{3,0},{4,5},{5,6},{6,7},{7,4},{8,9},{9,10},{10,1... | collective-permute-start | bytes 331784 | tf_op jit(solution)/shard_map/ppermute | solution.py:560
  120.7 5.2 %collective-permute-start.5 = (bf16[216,256]{1,0:T(8,128)(2,1)S(1)}, bf16[216,256]{1,0:T(8,128)(2,1)S(1)}, u32[]{:S(2)}, u32[]{:S(2)}) collective-permute-start(bf16[216,256]{1,0:T(8,128)(2,1)S(1)} %collective-permute-done.4.third_ref), channel_id=1, source_target_pairs={{0,3},{1,0},{2,1},{3,2},{4,7},{5,4},{6,5},{7,6},{8,11},{9,8},{10,9... | collective-permute-start | bytes 331784 | tf_op jit(solution)/shard_map/ppermute | solution.py:560

commit v4 on v0

--- a/solution.py
+++ b/solution.py
@@ -396,7 +396,7 @@
     up = mul(spread, head_tile(head, h))
     bias_lines = [None] * LAYERS
     for k in reversed(range(LAYERS)):
-        pre_grad = jnp.where(acts_ref[k].astype(F32) > 0, up, 0.0).astype(BF16)
+        pre_grad = jnp.where(acts_ref[k] > 0, up.astype(BF16), jnp.zeros((), BF16))
         bias_lines[k] = jnp.sum(pre_grad.astype(F32), axis=0, keepdims=True)
         if k > 0:
             start = ENC_WIDTH + (k - 1) * NET_WIDTH

time: 130 us -> 130 us (level)
  no operation moved by 1% of the time
where the time goes in v4:
time: 130 us; the launch traced here: 128 us
  blocking collectives  50.8 us (39%)
  Pallas kernels  37.9 us (29%)
  starting transfers between devices  24 us (18%)
  waiting for transfers between devices  14.4 us (11%)
    all_to_all x1, blocking collectives, shards(): lax.all_to_all(outgoing, 'expert', split_axis=0, concat_axis=0, tiled=True)  35.2 us
    ppermute x12, starting transfers between devices, send(): lax.ppermute(value, 'dp', [(i, (i + distance) % copies) for i in range(co...  18.4 us
    all_to_all x1, blocking collectives, shards(): lax.all_to_all(raw_out, 'expert', split_axis=0, concat_axis=0, tiled=True)  15.6 us
    pallas_call x2, Pallas kernels, gradient(): pl.pallas_call(functools.partial(backward_kernel, h), grid_spec=pltpu.Pre...  14 us
    all_to_all x1, waiting for transfers between devices, shards(): lax.all_to_all(cot_out, 'expert', split_axis=0, concat_axis=0, tiled=True)  9.98 us
    pallas_call x1, Pallas kernels, shards(): pl.pallas_call(dispatch_kernel, out_shape=shape_of((places, THIRDS * 128)...  7.21 us
    pallas_call x2, Pallas kernels, update(): pl.pallas_call(adam_kernel, grid_spec=pltpu.PrefetchScalarGridSpec(num_sc...  5.79 us
    all_to_all x1, starting transfers between devices, shards(): lax.all_to_all(cot_out, 'expert', split_axis=0, concat_axis=0, tiled=True)  5.62 us
  transfers between devices with their start and end apart: 13, of which 4 were waited for; matrix products, arithmetic and copies ran while one was open for 0% of the time, Pallas kernels for 8%

profile of v4, /device:TPU:2, one launch (start us, length us, event | category | flops | bytes accessed | tf_op | source)
XLA Modules:
  0.0 128.1 jit_solution(12559698586809399228)
XLA Ops:
  0.6 0.0 copy-start
  0.6 7.2 %dispatch.1 = bf16[1024,384]{1,0:T(8,128)(2,1)} custom-call(bf16[32,64,128]{2,1,0:T(8,128)(2,1)} %bitcast.20, s32[32,128]{1,0:T(8,128)} %bitcast.12, s32[32,128]{1,0:T(8,128)} %bitcast.14), custom_call_target="tpu_custom_call" | custom-call | tf_op jit(solution)/shard_map/dispatch/pallas_call | solution.py:482
  7.9 35.2 %all_to_all.21 = bf16[64,16,384]{2,1,0:T(8,128)(2,1)S(1)} all-to-all(bf16[64,16,384]{2,1,0:T(8,128)(2,1)} %bitcast.19), channel_id=1, replica_groups=mesh['expert'=64,'dp'=4] {'expert'}, dimensions={0} | all-to-all | bytes 1572864 | tf_op jit(solution)/shard_map/all_to_all | solution.py:497
  43.1 0.0 copy-start.7
  43.1 0.0 copy-start.8
  43.1 0.0 copy-start.9
  43.1 0.0 copy-start.10
  43.1 0.0 copy-start.11
  43.1 0.0 copy-done
  43.1 5.5 %forward.1 = (bf16[4,3072,256]{2,1,0:T(8,128)(2,1)}, bf16[4,3072,256]{2,1,0:T(8,128)(2,1)}, bf16[64,8,128]{2,1,0:T(8,128)(2,1)S(1)}, bf16[2,848,256]{2,1,0:T(8,128)(2,1)S(1)}) custom-call(bf16[1024,384]{1,0:T(8,128)(2,1)S(1)} %bitcast.9, f32[2,848,256]{2,1,0:T(8,128)S(1)} %copy-done), custom_call_target="tpu_custom_call" | custom-call | tf_op jit(solution)/shard_map/forward/pallas_call | solution.py:503
  48.7 15.6 %all_to_all.22.back_ref = bf16[64,8,128]{2,1,0:T(8,128)(2,1)S(1)} all-to-all(bf16[64,8,128]{2,1,0:T(8,128)(2,1)S(1)} %get-tuple-element.30), channel_id=1, replica_groups=mesh['expert'=64,'dp'=4] {'expert'}, dimensions={0} | all-to-all | bytes 262144 | tf_op jit(solution)/shard_map/all_to_all | solution.py:520
  64.3 0.0 copy-done.3
  64.3 0.0 copy-done.4
  64.3 0.0 copy-done.5
  64.3 0.0 copy-done.6
  64.3 5.4 %rays.1 = (bf16[64,8,128]{2,1,0:T(8,128)(2,1)}, f32[1,128]{1,0:T(1,128)}, f32[16,64]{1,0:T(8,128)}, f32[16,64]{1,0:T(8,128)}, f32[16,64]{1,0:T(8,128)}) custom-call(bf16[64,8,128]{2,1,0:T(8,128)(2,1)S(1)} %all_to_all.22.back_ref, s32[32,128]{1,0:T(8,128)S(1)} %bitcast.13, s32[32,128]{1,0:T(8,128)S(1)} %bitcast.15, s32[1,128]{1,0:T(1,128)S(1)} %bitcast.17, ...), custom_call_target="tpu_custom_call" | custom-call | tf_op jit(solution)/shard_map/rays/pallas_call | solution.py:523
  69.7 5.6 %all-to-all-start.2 = ((bf16[64,8,128]{2,1,0:T(8,128)(2,1)}), bf16[64,8,128]{2,1,0:T(8,128)(2,1)S(1)}, u32[]{:S(2)}, u32[]{:S(2)}) async-start(bf16[64,8,128]{2,1,0:T(8,128)(2,1)} %get-tuple-element.33), calls=%async_computation.2 | async-start | bytes 262144 | tf_op jit(solution)/shard_map/all_to_all | solution.py:551
  75.4 10.0 %all-to-all-done.2.cot_in_ref = bf16[64,8,128]{2,1,0:T(8,128)(2,1)S(1)} async-done(((bf16[64,8,128]{2,1,0:T(8,128)(2,1)}), bf16[64,8,128]{2,1,0:T(8,128)(2,1)S(1)}, u32[]{:S(2)}, u32[]{:S(2)}) %all-to-all-start.2) | async-done | bytes 131104 | tf_op jit(solution)/shard_map/all_to_all | solution.py:551
  85.4 6.8 %backward.3 = (f32[216,256]{1,0:T(8,128)S(1)}, bf16[216,256]{1,0:T(8,128)(2,1)S(1)}, bf16[216,256]{1,0:T(8,128)(2,1)S(1)}, bf16[216,256]{1,0:T(8,128)(2,1)S(1)}) custom-call(s32[4]{0:T(128)S(1)} %and_select_fusion.order_ref, bf16[1024,384]{1,0:T(8,128)(2,1)S(1)} %bitcast.10, bf16[4,3072,256]{2,1,0:T(8,128)(2,1)} %get-tuple-element.39.acts_ref, ...), custom_call_target="tpu_custom_call" | custom-call | flops 6000000000 | bytes 18000000 | tf_op jit(solution)/shard_map/backward/pallas_call | solution.py:563
  92.2 3.3 %collective-permute-start.6 = (bf16[216,256]{1,0:T(8,128)(2,1)S(1)}, bf16[216,256]{1,0:T(8,128)(2,1)S(1)}, u32[]{:S(2)}, u32[]{:S(2)}) collective-permute-start(bf16[216,256]{1,0:T(8,128)(2,1)S(1)} %get-tuple-element.41), channel_id=1, source_target_pairs={{0,2},{1,3},{2,0},{3,1},{4,6},{5,7},{6,4},{7,5},{8,10},{9,11},{10,... | collective-permute-start | bytes 331784 | tf_op jit(solution)/shard_map/ppermute | solution.py:560
  95.5 0.7 collective-permute-start.7
  96.1 2.6 %collective-permute-start.8 = (bf16[216,256]{1,0:T(8,128)(2,1)S(1)}, bf16[216,256]{1,0:T(8,128)(2,1)S(1)}, u32[]{:S(2)}, u32[]{:S(2)}) collective-permute-start(bf16[216,256]{1,0:T(8,128)(2,1)S(1)} %get-tuple-element.43), channel_id=1, source_target_pairs={{0,3},{1,0},{2,1},{3,2},{4,7},{5,4},{6,5},{7,6},{8,11},{9,8},{10,9... | collective-permute-start | bytes 331784 | tf_op jit(solution)/shard_map/ppermute | solution.py:560
  98.7 7.1 %backward.2 = (f32[216,256]{1,0:T(8,128)S(1)}, bf16[216,256]{1,0:T(8,128)(2,1)S(1)}, bf16[216,256]{1,0:T(8,128)(2,1)S(1)}, bf16[216,256]{1,0:T(8,128)(2,1)S(1)}) custom-call(s32[4]{0:T(128)S(1)} %and_select_fusion.order_ref, bf16[1024,384]{1,0:T(8,128)(2,1)S(1)} %bitcast.11, bf16[4,3072,256]{2,1,0:T(8,128)(2,1)} %get-tuple-element.32.acts_ref, ...), custom_call_target="tpu_custom_call" | custom-call | flops 6000000000 | bytes 18000000 | tf_op jit(solution)/shard_map/backward/pallas_call | solution.py:563
  105.8 0.1 collective-permute-start
  105.9 0.8 collective-permute-start.1
  106.8 0.0 collective-permute-done.6
  106.8 2.5 %collective-permute-start.2 = (bf16[216,256]{1,0:T(8,128)(2,1)S(1)}, bf16[216,256]{1,0:T(8,128)(2,1)S(1)}, u32[]{:S(2)}, u32[]{:S(2)}) collective-permute-start(bf16[216,256]{1,0:T(8,128)(2,1)S(1)} %get-tuple-element.38), channel_id=1, source_target_pairs={{0,3},{1,0},{2,1},{3,2},{4,7},{5,4},{6,5},{7,6},{8,11},{9,8},{10,9... | collective-permute-start | bytes 331784 | tf_op jit(solution)/shard_map/ppermute | solution.py:560
  109.3 0.0 collective-permute-done.7
  109.3 0.0 collective-permute-done.8
  109.3 0.1 add_convert_fusion.own_ref
  109.3 0.9 collective-permute-start.10
  110.2 1.2 collective-permute-start.9
  111.4 1.9 %collective-permute-done = bf16[216,256]{1,0:T(8,128)(2,1)S(1)} collective-permute-done((bf16[216,256]{1,0:T(8,128)(2,1)S(1)}, bf16[216,256]{1,0:T(8,128)(2,1)S(1)}, u32[]{:S(2)}, u32[]{:S(2)}) %collective-permute-start) | collective-permute-done | bytes 110624 | tf_op jit(solution)/shard_map/ppermute | solution.py:560
  113.4 1.1 collective-permute-done.1
  114.4 0.0 collective-permute-done.2
  114.4 0.1 add_convert_fusion.1.own_ref
  114.5 1.8 %collective-permute-start.4 = (bf16[216,256]{1,0:T(8,128)(2,1)S(1)}, bf16[216,256]{1,0:T(8,128)(2,1)S(1)}, u32[]{:S(2)}, u32[]{:S(2)}) collective-permute-start(bf16[216,256]{1,0:T(8,128)(2,1)S(1)} %add_convert_fusion.1.own_ref), channel_id=1, source_target_pairs={{0,3},{1,0},{2,1},{3,2},{4,7},{5,4},{6,5},{7,6},{8,11},{9,8},{10,9... | collective-permute-start | bytes 331784 | tf_op jit(solution)/shard_map/ppermute | solution.py:560
  116.3 0.0 collective-permute-done.10.third_ref
  116.3 0.8 collective-permute-start.11
  117.2 1.2 collective-permute-start.3
  118.4 1.4 %collective-permute-done.4.third_ref = bf16[216,256]{1,0:T(8,128)(2,1)S(1)} collective-permute-done((bf16[216,256]{1,0:T(8,128)(2,1)S(1)}, bf16[216,256]{1,0:T(8,128)(2,1)S(1)}, u32[]{:S(2)}, u32[]{:S(2)}) %collective-permute-start.4) | collective-permute-done | bytes 110624 | tf_op jit(solution)/shard_map/ppermute | solution.py:560
  119.8 2.5 %collective-permute-start.5 = (bf16[216,256]{1,0:T(8,128)(2,1)S(1)}, bf16[216,256]{1,0:T(8,128)(2,1)S(1)}, u32[]{:S(2)}, u32[]{:S(2)}) collective-permute-start(bf16[216,256]{1,0:T(8,128)(2,1)S(1)} %collective-permute-done.4.third_ref), channel_id=1, source_target_pairs={{0,3},{1,0},{2,1},{3,2},{4,7},{5,4},{6,5},{7,6},{8,11},{9,8},{10,9... | collective-permute-start | bytes 331784 | tf_op jit(solution)/shard_map/ppermute | solution.py:560
  122.3 0.0 collective-permute-done.9.first_ref
  122.3 0.0 collective-permute-done.11.second_ref
  122.3 2.9 %adam.2 = (f32[2,848,256]{2,1,0:T(8,128)}, f32[2,848,256]{2,1,0:T(8,128)}, f32[2,848,256]{2,1,0:T(8,128)}) custom-call(s32[4]{0:T(128)S(1)} %and_select_fusion.1.order_ref, bf16[216,256]{1,0:T(8,128)(2,1)S(1)} %add_convert_fusion.own_ref, bf16[216,256]{1,0:T(8,128)(2,1)S(1)} %collective-permute-done.9.first_ref, ...), custom_call_target="tpu_custom_call" | custom-call | flops 2000000000 | bytes 6000000 | tf_op jit(solution)/shard_map/adam/pallas_call | solution.py:597
  125.2 0.0 collective-permute-done.3.first_ref
  125.2 0.0 collective-permute-done.5.second_ref
  125.2 2.9 %adam.3 = (f32[2,848,256]{2,1,0:T(8,128)}, f32[2,848,256]{2,1,0:T(8,128)}, f32[2,848,256]{2,1,0:T(8,128)}) custom-call(s32[4]{0:T(128)S(1)} %and_select_fusion.1.order_ref, bf16[216,256]{1,0:T(8,128)(2,1)S(1)} %add_convert_fusion.1.own_ref, ...), custom_call_target="tpu_custom_call", output_to_operand_aliasing={{0}: (8, {}), {1}: (9, {}), {2}: (10, {})} | custom-call | flops 2000000000 | bytes 6000000 | tf_op jit(solution)/shard_map/adam/pallas_call | solution.py:597
  (15 shorter events, 0.0 us)
Async XLA Ops:
  0.6 42.5 %copy-start = (f32[2,848,256]{2,1,0:T(8,128)S(1)}, f32[2,848,256]{2,1,0:T(8,128)}, u32[]{:S(2)}) copy-start(f32[2,848,256]{2,1,0:T(8,128)} %param_ref.3) | copy-start | bytes 5210116
  43.1 21.2 %copy-start.3 = (s32[128,32]{0,1:T(8,128)S(1)}, s32[128,32]{0,1:T(8,128)}, u32[]{:S(2)}) copy-start(s32[128,32]{0,1:T(8,128)} %param.17) | copy-start | bytes 49156
  43.1 21.2 %copy-start.4 = (s32[128,32]{0,1:T(8,128)S(1)}, s32[128,32]{0,1:T(8,128)}, u32[]{:S(2)}) copy-start(s32[128,32]{0,1:T(8,128)} %param.18) | copy-start | bytes 49156
  43.1 21.2 %copy-start.5 = (f32[128,32]{0,1:T(8,128)S(1)}, f32[128,32]{0,1:T(8,128)}, u32[]{:S(2)}) copy-start(f32[128,32]{0,1:T(8,128)} %param.14) | copy-start | bytes 49156
  43.1 21.2 %copy-start.6 = (f32[16,64]{1,0:T(8,128)S(1)}, f32[16,64]{1,0:T(8,128)}, u32[]{:S(2)}) copy-start(f32[16,64]{1,0:T(8,128)} %code_ref.1) | copy-start | bytes 12292
  43.1 21.2 %copy-start.7 = (f32[16,64]{1,0:T(8,128)S(1)}, f32[16,64]{1,0:T(8,128)}, u32[]{:S(2)}) copy-start(f32[16,64]{1,0:T(8,128)} %first_ref.1) | copy-start | bytes 12292
  43.1 21.2 %copy-start.8 = (f32[16,64]{1,0:T(8,128)S(1)}, f32[16,64]{1,0:T(8,128)}, u32[]{:S(2)}) copy-start(f32[16,64]{1,0:T(8,128)} %second_ref.1) | copy-start | bytes 12292
  43.1 21.2 %copy-start.9 = (f32[3,128]{1,0:T(4,128)S(1)}, f32[3,128]{1,0:T(4,128)}, u32[]{:S(2)}) copy-start(f32[3,128]{1,0:T(4,128)} %targets_ref.1) | copy-start | bytes 4612
  43.1 21.2 %copy-start.10 = (s32[128]{0:T(128)S(1)}, s32[128]{0:T(128)}, u32[]{:S(2)}) copy-start(s32[128]{0:T(128)} %param.19) | copy-start | bytes 1540
  43.1 21.2 %copy-start.11 = (s32[128]{0:T(128)S(1)}, s32[128]{0:T(128)}, u32[]{:S(2)}) copy-start(s32[128]{0:T(128)} %param.16) | copy-start | bytes 1540
  69.7 15.6 %all-to-all-start.2 = ((bf16[64,8,128]{2,1,0:T(8,128)(2,1)}), bf16[64,8,128]{2,1,0:T(8,128)(2,1)S(1)}, u32[]{:S(2)}, u32[]{:S(2)}) async-start(bf16[64,8,128]{2,1,0:T(8,128)(2,1)} %get-tuple-element.33), calls=%async_computation.2 | async-start | bytes 262144 | tf_op jit(solution)/shard_map/all_to_all | solution.py:551
  92.2 14.6 %collective-permute-start.6 = (bf16[216,256]{1,0:T(8,128)(2,1)S(1)}, bf16[216,256]{1,0:T(8,128)(2,1)S(1)}, u32[]{:S(2)}, u32[]{:S(2)}) collective-permute-start(bf16[216,256]{1,0:T(8,128)(2,1)S(1)} %get-tuple-element.41), channel_id=1, source_target_pairs={{0,2},{1,3},{2,0},{3,1},{4,6},{5,7},{6,4},{7,5},{8,10},{9,11},{10,... | collective-permute-start | bytes 331784 | tf_op jit(solution)/shard_map/ppermute | solution.py:560
  95.5 13.8 %collective-permute-start.7 = (bf16[216,256]{1,0:T(8,128)(2,1)S(1)}, bf16[216,256]{1,0:T(8,128)(2,1)S(1)}, u32[]{:S(2)}, u32[]{:S(2)}) collective-permute-start(bf16[216,256]{1,0:T(8,128)(2,1)S(1)} %get-tuple-element.42), channel_id=1, source_target_pairs={{0,1},{1,2},{2,3},{3,0},{4,5},{5,6},{6,7},{7,4},{8,9},{9,10},{10,1... | collective-permute-start | bytes 331784 | tf_op jit(solution)/shard_map/ppermute | solution.py:560
  96.1 13.1 %collective-permute-start.8 = (bf16[216,256]{1,0:T(8,128)(2,1)S(1)}, bf16[216,256]{1,0:T(8,128)(2,1)S(1)}, u32[]{:S(2)}, u32[]{:S(2)}) collective-permute-start(bf16[216,256]{1,0:T(8,128)(2,1)S(1)} %get-tuple-element.43), channel_id=1, source_target_pairs={{0,3},{1,0},{2,1},{3,2},{4,7},{5,4},{6,5},{7,6},{8,11},{9,8},{10,9... | collective-permute-start | bytes 331784 | tf_op jit(solution)/shard_map/ppermute | solution.py:560
  98.7 23.6 %copy-start.1 = (f32[2,848,256]{2,1,0:T(8,128)S(1)}, f32[2,848,256]{2,1,0:T(8,128)}, u32[]{:S(2)}) copy-start(f32[2,848,256]{2,1,0:T(8,128)} %one_ref.3) | copy-start | bytes 5210116
  98.7 23.6 %copy-start.2 = (f32[2,848,256]{2,1,0:T(8,128)S(1)}, f32[2,848,256]{2,1,0:T(8,128)}, u32[]{:S(2)}) copy-start(f32[2,848,256]{2,1,0:T(8,128)} %two_ref.3) | copy-start | bytes 5210116
  105.8 7.5 %collective-permute-start = (bf16[216,256]{1,0:T(8,128)(2,1)S(1)}, bf16[216,256]{1,0:T(8,128)(2,1)S(1)}, u32[]{:S(2)}, u32[]{:S(2)}) collective-permute-start(bf16[216,256]{1,0:T(8,128)(2,1)S(1)} %get-tuple-element.36), channel_id=1, source_target_pairs={{0,2},{1,3},{2,0},{3,1},{4,6},{5,7},{6,4},{7,5},{8,10},{9,11},{10,... | collective-permute-start | bytes 331784 | tf_op jit(solution)/shard_map/ppermute | solution.py:560
  105.9 8.5 %collective-permute-start.1 = (bf16[216,256]{1,0:T(8,128)(2,1)S(1)}, bf16[216,256]{1,0:T(8,128)(2,1)S(1)}, u32[]{:S(2)}, u32[]{:S(2)}) collective-permute-start(bf16[216,256]{1,0:T(8,128)(2,1)S(1)} %get-tuple-element.37), channel_id=1, source_target_pairs={{0,1},{1,2},{2,3},{3,0},{4,5},{5,6},{6,7},{7,4},{8,9},{9,10},{10,1... | collective-permute-start | bytes 331784 | tf_op jit(solution)/shard_map/ppermute | solution.py:560
  106.8 7.6 %collective-permute-start.2 = (bf16[216,256]{1,0:T(8,128)(2,1)S(1)}, bf16[216,256]{1,0:T(8,128)(2,1)S(1)}, u32[]{:S(2)}, u32[]{:S(2)}) collective-permute-start(bf16[216,256]{1,0:T(8,128)(2,1)S(1)} %get-tuple-element.38), channel_id=1, source_target_pairs={{0,3},{1,0},{2,1},{3,2},{4,7},{5,4},{6,5},{7,6},{8,11},{9,8},{10,9... | collective-permute-start | bytes 331784 | tf_op jit(solution)/shard_map/ppermute | solution.py:560
  109.3 7.0 %collective-permute-start.10 = (bf16[216,256]{1,0:T(8,128)(2,1)S(1)}, bf16[216,256]{1,0:T(8,128)(2,1)S(1)}, u32[]{:S(2)}, u32[]{:S(2)}) collective-permute-start(bf16[216,256]{1,0:T(8,128)(2,1)S(1)} %add_convert_fusion.own_ref), channel_id=1, source_target_pairs={{0,3},{1,0},{2,1},{3,2},{4,7},{5,4},{6,5},{7,6},{8,11},{9,8},{10,9... | collective-permute-start | bytes 331784 | tf_op jit(solution)/shard_map/ppermute | solution.py:560
  110.2 12.0 %collective-permute-start.9 = (bf16[216,256]{1,0:T(8,128)(2,1)S(1)}, bf16[216,256]{1,0:T(8,128)(2,1)S(1)}, u32[]{:S(2)}, u32[]{:S(2)}) collective-permute-start(bf16[216,256]{1,0:T(8,128)(2,1)S(1)} %add_convert_fusion.own_ref), channel_id=1, source_target_pairs={{0,1},{1,2},{2,3},{3,0},{4,5},{5,6},{6,7},{7,4},{8,9},{9,10},{10,1... | collective-permute-start | bytes 331784 | tf_op jit(solution)/shard_map/ppermute | solution.py:560
  114.5 5.3 %collective-permute-start.4 = (bf16[216,256]{1,0:T(8,128)(2,1)S(1)}, bf16[216,256]{1,0:T(8,128)(2,1)S(1)}, u32[]{:S(2)}, u32[]{:S(2)}) collective-permute-start(bf16[216,256]{1,0:T(8,128)(2,1)S(1)} %add_convert_fusion.1.own_ref), channel_id=1, source_target_pairs={{0,3},{1,0},{2,1},{3,2},{4,7},{5,4},{6,5},{7,6},{8,11},{9,8},{10,9... | collective-permute-start | bytes 331784 | tf_op jit(solution)/shard_map/ppermute | solution.py:560
  116.3 6.0 %collective-permute-start.11 = (bf16[216,256]{1,0:T(8,128)(2,1)S(1)}, bf16[216,256]{1,0:T(8,128)(2,1)S(1)}, u32[]{:S(2)}, u32[]{:S(2)}) collective-permute-start(bf16[216,256]{1,0:T(8,128)(2,1)S(1)} %collective-permute-done.10.third_ref), channel_id=1, source_target_pairs={{0,3},{1,0},{2,1},{3,2},{4,7},{5,4},{6,5},{7,6},{8,11},{9,8},{10,9... | collective-permute-start | bytes 331784 | tf_op jit(solution)/shard_map/ppermute | solution.py:560
  117.2 8.0 %collective-permute-start.3 = (bf16[216,256]{1,0:T(8,128)(2,1)S(1)}, bf16[216,256]{1,0:T(8,128)(2,1)S(1)}, u32[]{:S(2)}, u32[]{:S(2)}) collective-permute-start(bf16[216,256]{1,0:T(8,128)(2,1)S(1)} %add_convert_fusion.1.own_ref), channel_id=1, source_target_pairs={{0,1},{1,2},{2,3},{3,0},{4,5},{5,6},{6,7},{7,4},{8,9},{9,10},{10,1... | collective-permute-start | bytes 331784 | tf_op jit(solution)/shard_map/ppermute | solution.py:560
  119.8 5.4 %collective-permute-start.5 = (bf16[216,256]{1,0:T(8,128)(2,1)S(1)}, bf16[216,256]{1,0:T(8,128)(2,1)S(1)}, u32[]{:S(2)}, u32[]{:S(2)}) collective-permute-start(bf16[216,256]{1,0:T(8,128)(2,1)S(1)} %collective-permute-done.4.third_ref), channel_id=1, source_target_pairs={{0,3},{1,0},{2,1},{3,2},{4,7},{5,4},{6,5},{7,6},{8,11},{9,8},{10,9... | collective-permute-start | bytes 331784 | tf_op jit(solution)/shard_map/ppermute | solution.py:560
